TPU v7x, 128 devices: a whole 4x4x4 slice. The times are simulated.
128 devices in a mesh: blk: 16 (over x, z_lo, core), smp: 8 (over y, z_hi).
Axes of the slice: x: 4, y: 4, z: 4 (z_hi: 2, z_lo: 2; z = z_hi * 2 + z_lo), core: 2. Of those that a mesh axis runs over, the one named last changes fastest.
Arguments:
- scaled_genotype_counts: bfloat16 [16384, 8192], P('smp', 'blk'), may hold values from -6 to 6
- adjusted_trait_scores: bfloat16 [16384, 8], P('smp'), may hold values from -6 to 6
- subset_membership: int32 [16384], P('smp'), may hold values from 0 to 4, as said below
- regularizer_lambdas: float32 [2], replicated, may hold values from 0.01 to 0.1
- unseen_subset_guesses: bfloat16 [8, 2048, 8, 32], P('smp', 'blk'), may hold values from -6 to 6
Outputs:
- oof: bfloat16 [16384, 8, 32], P('smp', None, 'blk')
- cross: float32 [8, 32, 64], P(None, 'blk', 'smp')
Inputs may be any that keep to these rules, and one draw needn't show every extreme that they name: `subset_membership`: every fold holds some samples.
All inputs are finite; a program needn't handle non-finite values.
Results may differ from a plain program's by a relative error of at most 0.0047.
Values may be sent and summed in bfloat16 or wider, within the bound.
A program may use at most 128 MiB of HBM per device.

v0:
```python
import math

import jax
import jax.numpy as jnp
from jax import lax
from jax.sharding import PartitionSpec as P

BLOCK = 512
PHENOTYPIC_MEASURES = 8
FOLDS = 5
SHRINK_STRENGTH = 2


def fold_sums(locus_group_span, adjusted_trait_scores, partition_indicator):
    masked_values = locus_group_span[:, None, :] * partition_indicator[:, :, None]
    inner_covariance_stack = jnp.einsum(
        "rpe,ro->peo", masked_values, locus_group_span, preferred_element_type=jnp.float32
    )
    pairwise_interaction_features = jnp.einsum(
        "jdx,jr->dxr", masked_values, adjusted_trait_scores, preferred_element_type=jnp.float32
    )
    return (inner_covariance_stack, pairwise_interaction_features)


def invert_all_equations(
    normal_equation_stack, equation_targets, regularizer_lambdas, person_entries
):
    unit_diagonal = jnp.eye(BLOCK, dtype=jnp.float32)
    solved = []
    for position_number in range(SHRINK_STRENGTH):
        regressor_array = (
            normal_equation_stack
            + regularizer_lambdas[position_number] * person_entries * unit_diagonal
        )
        factor = jnp.linalg.cholesky(regressor_array)
        solved.append(
            jax.vmap(lambda c, b: jax.scipy.linalg.cho_solve((c, True), b))(
                factor, equation_targets
            )
        )
    return jnp.stack(solved, axis=-1)


def predict_output(
    locus_group_span,
    inner_covariance_stack,
    pairwise_interaction_features,
    partition_indicator,
    regularizer_lambdas,
    person_entries,
):
    normal_equation_stack = jnp.sum(inner_covariance_stack, axis=0)[None] - inner_covariance_stack
    equation_targets = (
        jnp.sum(pairwise_interaction_features, axis=0)[None] - pairwise_interaction_features
    )
    weight_array = invert_all_equations(
        normal_equation_stack, equation_targets, regularizer_lambdas, person_entries
    )
    coeffs_half = jnp.transpose(weight_array, (1, 0, 2, 3)).astype(jnp.bfloat16)
    fitted = jnp.dot(
        locus_group_span, coeffs_half.reshape(BLOCK, -1), preferred_element_type=jnp.float32
    )
    fitted = fitted.reshape(locus_group_span.shape[0], FOLDS, PHENOTYPIC_MEASURES, SHRINK_STRENGTH)
    chosen = jnp.sum(fitted * partition_indicator.astype(jnp.float32)[:, :, None, None], axis=1)
    return (chosen * math.sqrt(person_entries / BLOCK)).astype(jnp.bfloat16)


def local(
    scaled_genotype_counts,
    adjusted_trait_scores,
    subset_membership,
    regularizer_lambdas,
    unseen_subset_guesses,
):
    rows = scaled_genotype_counts.shape[0]
    person_entries = rows * lax.axis_size("smp")
    scale = 1.0 / person_entries
    partial_pieces = [scaled_genotype_counts]
    partition_indicator = (
        subset_membership[:, None] == jnp.arange(FOLDS, dtype=jnp.int32)[None, :]
    ).astype(jnp.bfloat16)
    sums = [
        fold_sums(piece, adjusted_trait_scores, partition_indicator) for piece in partial_pieces
    ]
    inner_covariance_stack = jnp.stack([item[0] for item in sums])
    pairwise_interaction_features = jnp.stack([item[1] for item in sums])
    inner_covariance_stack, pairwise_interaction_features = lax.psum(
        (inner_covariance_stack, pairwise_interaction_features), "smp"
    )
    fold_predictions = predict_output(
        partial_pieces[0],
        inner_covariance_stack[0],
        pairwise_interaction_features[0],
        partition_indicator,
        regularizer_lambdas,
        person_entries,
    )
    new_part = (
        jnp.einsum(
            "stf,stc->tfc",
            fold_predictions,
            lax.all_gather(fold_predictions, "blk", axis=2, tiled=True),
            preferred_element_type=jnp.float32,
        )
        * scale
    )
    old_part = (
        jnp.einsum(
            "stf,stc->tfc",
            fold_predictions,
            lax.all_gather(unseen_subset_guesses, "blk", axis=1, tiled=True)[0],
            preferred_element_type=jnp.float32,
        )
        * scale
    )
    partial_value = jnp.concatenate([old_part, new_part], axis=2)
    cross = lax.psum_scatter(partial_value, "smp", scatter_dimension=2, tiled=True)
    return (fold_predictions, cross)


def solution(mesh):
    return jax.shard_map(
        local,
        mesh=mesh,
        in_specs=(P("smp", "blk"), P("smp", None), P("smp"), P(), P("smp", "blk", None, None)),
        out_specs=(P("smp", None, "blk"), P(None, "blk", "smp")),
        check_vma=False,
    )
```

profile of v0, /device:TPU:1, one launch (start us, length us, event | category | flops | bytes accessed | tf_op | source)
XLA Modules:
  0.0 1642.0 jit_solution(17644328493073081873)
XLA Ops:
  9.4 11.6 fusion.12
  26.3 233.6 %all-reduce.5.cloned.1.call-done = (f32[1,5,512,512]{2,3,1,0:T(8,128)}, f32[1,5,512,8]{2,3,1,0:T(8,128)}) async-done(((f32[1,5,512,512]{2,3,1,0:T(8,128)}, f32[1,5,512,8]{2,3,1,0:T(8,128)}), (f32[1,5,512,512]{2,3,1,0:T(8,128)}, f32[1,5,512,8]{2,3,1,0:T(8,128)})) %all-reduce.5.cloned.1.call-update) | async-done | bytes 5324816 | tf_op jit(solution)/shard_map/psum | solution.py:87
  260.0 3.2 reduce_sum.27
  263.2 8.5 fusion.11
  271.7 6.1 copy.166
  277.8 5.9 copy.150
  283.7 13.6 fusion.4
  298.3 58.6 %custom-call.37 = f32[5,128,128]{2,1,0:T(8,128)S(1)} custom-call(f32[5,128,128]{2,1,0:T(8,128)S(1)} %cholesky.430), custom_call_target="Cholesky" | custom-call | tf_op jit(solution)/shard_map/jit(cholesky)/cholesky | solution.py:35
  356.9 3.0 cholesky.320
  360.0 49.1 %custom-call.38 = f32[5,1,128,128]{2,3,1,0:T(8,128)S(1)} custom-call(f32[5,1,128,128]{3,2,1,0:T(8,128)S(1)} %select_bitcast_fusion.5), custom_call_target="InvertDiagBlocksLowerTriangular" | custom-call | tf_op jit(solution)/shard_map/jit(cholesky)/cholesky | solution.py:35
  409.1 3.3 constant_dynamic-update-slice_fusion.7
  414.6 58.8 %custom-call.39 = f32[5,128,128]{2,1,0:T(8,128)S(1)} custom-call(f32[5,128,128]{2,1,0:T(8,128)S(1)} %cholesky.434), custom_call_target="Cholesky" | custom-call | tf_op jit(solution)/shard_map/jit(cholesky)/cholesky | solution.py:35
  474.3 49.1 %custom-call.40 = f32[5,1,128,128]{2,3,1,0:T(8,128)S(1)} custom-call(f32[5,1,128,128]{3,2,1,0:T(8,128)S(1)} %get-tuple-element.58), custom_call_target="InvertDiagBlocksLowerTriangular" | custom-call | tf_op jit(solution)/shard_map/jit(cholesky)/cholesky | solution.py:35
  528.0 58.6 %custom-call.41 = f32[5,128,128]{2,1,0:T(8,128)S(1)} custom-call(f32[5,128,128]{2,1,0:T(8,128)S(1)} %cholesky.439), custom_call_target="Cholesky" | custom-call | tf_op jit(solution)/shard_map/jit(cholesky)/cholesky | solution.py:35
  587.6 59.0 %custom-call.45 = f32[5,128,128]{2,1,0:T(8,128)S(1)} custom-call(f32[5,128,128]{2,1,0:T(8,128)S(1)} %cholesky.443), custom_call_target="Cholesky" | custom-call | tf_op jit(solution)/shard_map/jit(cholesky)/cholesky | solution.py:35
  647.5 49.1 %custom-call.42 = f32[5,1,128,128]{2,3,1,0:T(8,128)S(1)} custom-call(f32[5,1,128,128]{3,2,1,0:T(8,128)S(1)} %get-tuple-element.56), custom_call_target="InvertDiagBlocksLowerTriangular" | custom-call | tf_op jit(solution)/shard_map/jit(cholesky)/cholesky | solution.py:35
  700.8 58.6 %custom-call.43 = f32[5,128,128]{2,1,0:T(8,128)S(1)} custom-call(f32[5,128,128]{2,1,0:T(8,128)S(1)} %convolution_subtract_fusion.3), custom_call_target="Cholesky" | custom-call | tf_op jit(solution)/shard_map/jit(cholesky)/cholesky | solution.py:35
  762.4 49.3 %custom-call.46 = f32[5,1,128,128]{2,3,1,0:T(8,128)S(1)} custom-call(f32[5,1,128,128]{3,2,1,0:T(8,128)S(1)} %get-tuple-element.66), custom_call_target="InvertDiagBlocksLowerTriangular" | custom-call | tf_op jit(solution)/shard_map/jit(cholesky)/cholesky | solution.py:35
  811.7 3.2 constant_dynamic-update-slice_fusion.3
  817.8 59.4 %custom-call.47 = f32[5,128,128]{2,1,0:T(8,128)S(1)} custom-call(f32[5,128,128]{2,1,0:T(8,128)} %cholesky.447), custom_call_target="Cholesky" | custom-call | tf_op jit(solution)/shard_map/jit(cholesky)/cholesky | solution.py:35
  878.2 50.7 %custom-call.48 = f32[5,1,128,128]{2,3,1,0:T(8,128)} custom-call(f32[5,1,128,128]{3,2,1,0:T(8,128)} %get-tuple-element.62), custom_call_target="InvertDiagBlocksLowerTriangular" | custom-call | tf_op jit(solution)/shard_map/jit(cholesky)/cholesky | solution.py:35
  931.5 3.1 fusion.23
  935.3 59.4 %custom-call.49 = f32[5,128,128]{2,1,0:T(8,128)S(1)} custom-call(f32[5,128,128]{2,1,0:T(8,128)} %cholesky.452), custom_call_target="Cholesky" | custom-call | tf_op jit(solution)/shard_map/jit(cholesky)/cholesky | solution.py:35
  995.6 50.6 %custom-call.50 = f32[5,1,128,128]{2,3,1,0:T(8,128)} custom-call(f32[5,1,128,128]{3,2,1,0:T(8,128)} %get-tuple-element.60), custom_call_target="InvertDiagBlocksLowerTriangular" | custom-call | tf_op jit(solution)/shard_map/jit(cholesky)/cholesky | solution.py:35
  1051.4 59.0 %custom-call.51 = f32[5,128,128]{2,1,0:T(8,128)S(1)} custom-call(f32[5,128,128]{2,1,0:T(8,128)S(1)} %convolution_subtract_fusion.2), custom_call_target="Cholesky" | custom-call | tf_op jit(solution)/shard_map/jit(cholesky)/cholesky | solution.py:35
  1112.6 10.0 select_select_fusion.1
  1122.7 12.5 while.5
  1135.2 196.7 %custom-call.52 = f32[5,4,128,128]{2,3,1,0:T(8,128)S(1)} custom-call(f32[5,4,128,128]{3,2,1,0:T(8,128)S(1)} %bitcast.175), custom_call_target="InvertDiagBlocksLowerTriangular" | custom-call | tf_op jit(solution)/shard_map/vmap(jit(_cho_solve))/triangular_solve | solution.py:37
  1346.9 12.8 while.4
  1360.8 197.5 %custom-call.44 = f32[5,4,128,128]{2,3,1,0:T(8,128)S(1)} custom-call(f32[5,4,128,128]{3,2,1,0:T(8,128)} %bitcast.174), custom_call_target="InvertDiagBlocksLowerTriangular" | custom-call | tf_op jit(solution)/shard_map/vmap(jit(_cho_solve))/triangular_solve | solution.py:37
  1579.9 31.2 %all-gather.5.cloned.1.call-done = bf16[2048,8,32]{0,1,2:T(8,128)(2,1)} async-done(((bf16[2048,8,2]{0,1,2:T(8,128)(2,1)}), bf16[2048,8,32]{0,1,2:T(8,128)(2,1)}) %all-gather.5.cloned.1.call-update) | async-done | bytes 1048592 | tf_op jit(solution)/shard_map/all_gather | solution.py:102
  1613.1 20.5 %all-reduce.1 = f32[8,2,64]{2,1,0:T(2,128)S(1)} all-reduce(f32[8,2,64]{2,1,0:T(2,128)S(1)} %pad_maximum_fusion), channel_id=2, replica_groups=mesh['blk'=16,'smp'=8] {'smp'}, use_global_device_ids=true, to_apply=%region_13.16.clone | all-reduce | flops 1024 | bytes 8192
  (144 shorter events, 103.4 us)
Async XLA Ops:
  8.0 13.0 copy-start
  8.0 252.0 %all-reduce.5.cloned.1.call-start = ((), (), s32[]{:S(2)}) async-start(), calls=%async_computation.2 | async-start | bytes 10649600 | tf_op jit(solution)/shard_map/psum | solution.py:87
  9.4 11.6 copy-start.2
  23.5 0.8 copy-start.11
  23.5 1554.8 %all-gather.3.cloned.1.call-start = ((), (), s32[]{:S(2)}) async-start(), calls=%async_computation | async-start | bytes 1114112 | tf_op jit(solution)/shard_map/all_gather | solution.py:111
  24.1 1587.0 %all-gather.5.cloned.1.call-start = ((), (), s32[]{:S(2)}) async-start(), calls=%async_computation.1 | async-start | bytes 1114112 | tf_op jit(solution)/shard_map/all_gather | solution.py:102
  1112.6 219.3 %copy-start.5 = (f32[1,5,512,8]{2,3,1,0:T(8,128)S(1)}, f32[1,5,512,8]{2,3,1,0:T(8,128)}, u32[]{:S(2)}) copy-start(f32[1,5,512,8]{2,3,1,0:T(8,128)} %get-tuple-element.47) | copy-start | bytes 245764
  1341.9 5.0 copy-start.6
  1344.1 2.8 copy-start.9
  1346.9 226.3 %copy-start.3 = (bf16[2048,512]{1,0:T(8,128)(2,1)S(1)}, bf16[2048,512]{1,0:T(8,128)(2,1)}, u32[]{:S(2)}) copy-start(bf16[2048,512]{1,0:T(8,128)(2,1)} %param.8) | copy-start | bytes 6291460
  1359.7 1.1 copy-start.4
  1558.3 11.5 copy-start.7
  1558.3 11.5 copy-start.10
  1569.9 64.4 %copy-start.1 = (bf16[2048,8]{0,1:T(8,128)(2,1)S(1)}, bf16[2048,8]{0,1:T(8,128)(2,1)}, u32[]{:S(2)}) copy-start(bf16[2048,8]{0,1:T(8,128)(2,1)} %param.9) | copy-start | bytes 98308
  1575.7 58.6 %copy-start.8 = (bf16[2048,8,2]{0,2,1:T(2,128)(2,1)}, bf16[2048,8,2]{0,2,1:T(2,128)(2,1)S(1)}, u32[]{:S(2)}) copy-start(bf16[2048,8,2]{0,2,1:T(2,128)(2,1)S(1)} %multiply_convert_fusion) | copy-start | bytes 196612
Sparse Core Ops, SparseCore 0:
  23.7 236.2 all-reduce.4
Sparse Core Ops, SparseCore 1:
  25.7 72.4 all-gather.2
  1576.5 34.6 all-gather.4
where the time goes:
time: 1650 us; the launch traced here: 1640 us
  other arithmetic  1210 us (73%)
  waiting for transfers between devices  265 us (16%)
  matrix products  78.3 us (5%)
  local copies, waits for them, and re-layouts  51.8 us (3%)
  blocking collectives  20.5 us (1%)
  between operations  18 us (1%)
    another operation x32, other arithmetic, invert_all_equations(): factor = jnp.linalg.cholesky(regressor_array)  775 us
    another operation x5, other arithmetic, invert_all_equations(): jax.scipy.linalg.cho_solve((c, True), b)  404 us
    psum x1, waiting for transfers between devices, local(): lax.psum((inner_covariance_stack, pairwise_interaction_features), 'smp')  234 us
  transfers between devices with their start and end apart: 3, of which 2 were waited for; matrix products, arithmetic and copies ran while one was open for 80% of the time, Pallas kernels for 0%

commit v1 on v0

v1 whole, which is shorter than its diff:
```python
import math

import jax
import jax.numpy as jnp
from jax import lax
from jax.experimental import pallas as pl
from jax.experimental.pallas import tpu as pltpu
from jax.sharding import PartitionSpec as P

HI = lax.Precision.HIGHEST
NB = 4
BLK = [(p, q) for p in range(NB) for q in range(p, NB)]
IDX = {pq: i for i, pq in enumerate(BLK)}


def lanes(x, m):
    return jnp.broadcast_to(x[:, m:m + 1], x.shape)


def subl(x, m):
    return jnp.broadcast_to(x[m:m + 1, :], x.shape)


def sweep_step(groups):
    a0 = groups[0]
    lane = lax.broadcasted_iota(jnp.int32, (8, 128), 1)
    sub = lax.broadcasted_iota(jnp.int32, (8, 128), 0)
    cols = [lanes(a0, m) for m in range(8)]
    s = {(i, m): subl(cols[m], i) for m in range(8) for i in range(m, 8)}
    z = [jnp.where(lane < 8, jnp.where(lane == m, -1.0, 0.0), subl(a0, m)) for m in range(8)]
    d, l = [None] * 8, {}
    for m in range(8):
        d[m] = 1.0 / s[m, m]
        for i in range(m + 1, 8):
            l[i, m] = s[i, m] * d[m]
        for j in range(m + 1, 8):
            for i in range(j, 8):
                s[i, j] = s[i, j] - l[i, m] * s[j, m]
        for i in range(m + 1, 8):
            z[i] = z[i] - l[i, m] * z[m]
    q = [z[m] * d[m] for m in range(8)]
    for m in range(7, -1, -1):
        for i in range(m):
            q[i] = q[i] - l[m, i] * q[m]
    out = []
    for g in range(1, 16):
        a = groups[g]
        new = jnp.where(lane < 8, 0.0, a)
        for m in range(8):
            new = new - lanes(a, m) * q[m]
        out.append(pltpu.roll(new, 120, 1))
    new = q[0]
    for m in range(1, 8):
        new = jnp.where(sub == m, q[m], new)
    out.append(pltpu.roll(new, 120, 1))
    return out


def inverse(mats):
    def body(_, carry):
        return tuple(tuple(sweep_step(list(c))) for c in carry)
    init = tuple(tuple(m[8 * g:8 * g + 8, :] for g in range(16)) for m in mats)
    out = lax.fori_loop(0, 16, body, init)
    return [-jnp.concatenate(list(c), axis=0) for c in out]


def dot(a, b, ca=1, cb=0):
    return lax.dot_general(a, b, (((ca,), (cb,)), ((), ())), precision=HI, preferred_element_type=jnp.float32)


def solve_kernel(lam_ref, a_ref, b_ref, out_ref, s_ref, t_ref, y_ref, w_ref):
    n = 16384.0
    row = lax.broadcasted_iota(jnp.int32, (128, 128), 0)
    col = lax.broadcasted_iota(jnp.int32, (128, 128), 1)
    for j in range(2):
        shift = lam_ref[j] * n
        for p in range(NB):
            for q in range(p, NB):
                v = a_ref[IDX[p, q]]
                if p == q:
                    v = v + jnp.where(row == col, shift, 0.0)
                s_ref[j, p, :, 128 * q:128 * q + 128] = v
        y_ref[j] = b_ref[...]
    for p in range(NB):
        lo, hi = 128 * p, 128 * p + 128
        ws = inverse([s_ref[j, p, :, lo:hi] for j in range(2)])
        for j in range(2):
            w = ws[j]
            y = dot(y_ref[j, :, lo:hi], w)
            y_ref[j, :, lo:hi] = y
            if p + 1 < NB:
                right = s_ref[j, p, :, hi:]
                t = dot(w, right)
                t_ref[j, p, :, hi:] = t
                y_ref[j, :, hi:] = y_ref[j, :, hi:] - dot(y, right)
                for q in range(p + 1, NB):
                    k = 128 * q
                    s_ref[j, q, :, k:] = s_ref[j, q, :, k:] - dot(s_ref[j, p, :, k:k + 128], t_ref[j, p, :, k:], 0, 0)
    for j in range(2):
        for p in range(NB - 2, -1, -1):
            lo, hi = 128 * p, 128 * p + 128
            y_ref[j, :, lo:hi] = y_ref[j, :, lo:hi] - dot(y_ref[j, :, hi:], t_ref[j, p, :, hi:], 1, 1)
    for t in range(8):
        for j in range(2):
            out_ref[2 * t + j:2 * t + j + 1, :] = y_ref[j, t:t + 1, :]


def solve(lam, a, b):
    return pl.pallas_call(
        solve_kernel,
        out_shape=jax.ShapeDtypeStruct((16, 512), jnp.float32),
        in_specs=[pl.BlockSpec(memory_space=pltpu.SMEM), pl.BlockSpec(memory_space=pltpu.VMEM), pl.BlockSpec(memory_space=pltpu.VMEM)],
        out_specs=pl.BlockSpec(memory_space=pltpu.VMEM),
        scratch_shapes=[pltpu.VMEM((2, 4, 128, 512), jnp.float32), pltpu.VMEM((2, 4, 128, 512), jnp.float32), pltpu.VMEM((2, 8, 512), jnp.float32), pltpu.VMEM((2, 128, 128), jnp.float32)],
        compiler_params=pltpu.CompilerParams(vmem_limit_bytes=40 << 20),
    )(lam, a, b)


FOLDS = 5
BLOCK = 512
TRAITS = 8


def local(x, y, fold, lam, old):
    rows = x.shape[0]
    person_entries = rows * lax.axis_size("smp")
    scale = 1.0 / person_entries
    ind = (fold[:, None] == jnp.arange(FOLDS, dtype=jnp.int32)[None, :]).astype(jnp.bfloat16)
    masked = x[:, None, :] * ind[:, :, None]
    gram = jnp.einsum("rpe,ro->peo", masked, x, preferred_element_type=jnp.float32)
    xy = jnp.einsum("jdx,jr->drx", masked, y, preferred_element_type=jnp.float32)
    gram, xy = lax.psum((gram, xy), "smp")
    mine = jnp.minimum(lax.axis_index("smp"), FOLDS - 1)
    a = jnp.sum(gram, axis=0) - lax.dynamic_index_in_dim(gram, mine, 0, keepdims=False)
    b = jnp.sum(xy, axis=0) - lax.dynamic_index_in_dim(xy, mine, 0, keepdims=False)
    blocks = jnp.stack([a[128 * p:128 * p + 128, 128 * q:128 * q + 128] for p, q in BLK])
    beta = solve(lam, blocks, b).astype(jnp.bfloat16)
    betas = lax.all_gather(beta, "smp", axis=0)[:FOLDS].reshape(FOLDS * 16, BLOCK)
    fitted = lax.dot_general(betas, x, (((1,), (1,)), ((), ())), preferred_element_type=jnp.float32)
    fitted = fitted.reshape(FOLDS, 16, rows)
    chosen = jnp.zeros((16, rows), jnp.float32)
    for k in range(FOLDS):
        chosen = jnp.where(fold[None, :] == k, fitted[k], chosen)
    oof = (chosen * math.sqrt(person_entries / BLOCK)).astype(jnp.bfloat16).reshape(TRAITS, 2, rows)
    everyone = lax.all_gather(oof, "blk", axis=1, tiled=True)
    new_part = jnp.einsum("tfs,tcs->tfc", oof, everyone, preferred_element_type=jnp.float32)
    before = lax.all_gather(old, "blk", axis=1, tiled=True)[0]
    old_part = jnp.einsum("tfs,stc->tfc", oof, before, preferred_element_type=jnp.float32)
    partial_value = jnp.concatenate([old_part, new_part], axis=2) * scale
    cross = lax.psum_scatter(partial_value, "smp", scatter_dimension=2, tiled=True)
    return jnp.transpose(oof, (2, 0, 1)), cross


def solution(mesh):
    return jax.shard_map(
        local,
        mesh=mesh,
        in_specs=(P("smp", "blk"), P("smp", None), P("smp"), P(), P("smp", "blk", None, None)),
        out_specs=(P("smp", None, "blk"), P(None, "blk", "smp")),
        check_vma=False,
    )
```

time: 1650 us -> 481 us (0.29)
  other arithmetic: 1210 us -> 6.56 us
  Pallas kernels: 0 us -> 113 us
  matrix products: 78.3 us -> 19.4 us
  local copies, waits for them, and re-layouts: 51.8 us -> 3.38 us
  blocking collectives: 20.5 us -> 50 us
    another operation x39 -> x0, other arithmetic: 1180 us -> none  [the longest x32 775 us: invert_all_equations(): factor = jnp.linalg.cholesky(regressor_array)]
    pallas_call x0 -> x1, Pallas kernels: none -> 113 us  [solve(): pl.pallas_call(solve_kernel, out_shape=jax.ShapeDtypeStruct((16, 512), jn...]
    another operation x40 -> x0, matrix products: 59.9 us -> none  [the longest x12 30.5 us: invert_all_equations(): factor = jnp.linalg.cholesky(regressor_array)]
    another operation x35 -> x1, local copies, waits for them, and re-layouts: 35 us -> 0.01 us  [local(): jnp.stack([a[128 * p:128 * p + 128, 128 * q:128 * q + 128] for p, q in BLK])]
    all_gather x0 -> x1, blocking collectives: none -> 29.5 us  [local(): lax.all_gather(beta, 'smp', axis=0)[:FOLDS].reshape(FOLDS * 16, BLOCK)]
  transfers between devices with their start and end apart: 3 -> 3, of which waited for: 2 -> 2; matrix products, arithmetic and copies ran while one was open for 80% -> 3% of each run, Pallas kernels for 0% -> 24%
where the time goes in v1:
time: 481 us; the launch traced here: 478 us
  waiting for transfers between devices  269 us (56%)
  Pallas kernels  113 us (23%)
  blocking collectives  50 us (10%)
  matrix products  19.4 us (4%)
  between operations  16.4 us (3%)
  other arithmetic  6.56 us (1%)
    psum x1, waiting for transfers between devices, local(): gram, xy = lax.psum((gram, xy), 'smp')  236 us
    pallas_call x1, Pallas kernels, solve(): pl.pallas_call(solve_kernel, out_shape=jax.ShapeDtypeStruct((16, 512), jn...  113 us
    all_gather x1, waiting for transfers between devices, local(): everyone = lax.all_gather(oof, 'blk', axis=1, tiled=True)  33.2 us
    all_gather x1, blocking collectives, local(): lax.all_gather(beta, 'smp', axis=0)[:FOLDS].reshape(FOLDS * 16, BLOCK)  29.5 us
    unnamed x1, blocking collectives  20.5 us
    dot_general x1, matrix products, local(): jnp.einsum('rpe,ro->peo', masked, x, preferred_element_type=jnp.float32)  11.1 us
  transfers between devices with their start and end apart: 3, of which 2 were waited for; matrix products, arithmetic and copies ran while one was open for 3% of the time, Pallas kernels for 24%

profile of v1, /device:TPU:1, one launch (start us, length us, event | category | flops | bytes accessed | tf_op | source)
XLA Modules:
  0.0 478.0 jit_solution(1499193439990986462)
XLA Ops:
  8.0 0.0 copy-start
  8.0 0.0 all-reduce.4.cloned.1.call-start
  8.1 0.7 fusion.30
  8.8 11.1 %fusion.2 = f32[5,512,512]{2,1,0:T(8,128)} fusion(bf16[2048,5]{0,1:T(8,128)(2,1)S(1)} %fusion.30, bf16[2048,512]{1,0:T(8,128)(2,1)} %param.5), kind=kOutput, calls=%fused_computation.2 | convolution fusion | flops 5373952000 | bytes 7360512 | tf_op jit(solution)/shard_map/rpe,ro->peo/dot_general | solution.py:130
  19.9 2.4 fusion.9
  22.3 0.0 all-reduce.4.cloned.1.call-update
  22.3 0.0 all-gather.4.cloned.1.call-start
  22.4 0.5 all-gather.4.cloned.1.call-update
  22.9 0.2 all-gather.6.cloned.1.call-start
  23.2 235.6 %all-reduce.4.cloned.1.call-done = (f32[5,512,512]{2,1,0:T(8,128)}, f32[5,8,512]{2,1,0:T(8,128)}) async-done(((f32[5,512,512]{2,1,0:T(8,128)}, f32[5,8,512]{2,1,0:T(8,128)}), (f32[5,512,512]{2,1,0:T(8,128)}, f32[5,8,512]{2,1,0:T(8,128)})) %all-reduce.4.cloned.1.call-update) | async-done | bytes 5324816 | tf_op jit(solution)/shard_map/psum | solution.py:132
  258.7 3.3 reduce_sum.18
  262.0 0.0 copy-start.5
  262.0 1.4 bitcast_subtract_fusion
  263.7 112.6 %shard_map.68 = f32[16,512]{1,0:T(8,128)S(1)} custom-call(f32[2]{0:T(128)S(1)} %copy-done.1, f32[10,128,128]{2,1,0:T(8,128)S(1)} %fusion.20.a_ref, f32[8,512]{1,0:T(8,128)S(1)} %bitcast_subtract_fusion.1.b_ref), custom_call_target="tpu_custom_call" | custom-call | tf_op jit(solution)/shard_map/pallas_call | solution.py:109
  376.4 29.5 %all-gather = bf16[128,512]{1,0:T(8,128)(2,1)S(1)} all-gather(bf16[16,512]{1,0:T(8,128)(2,1)S(1)} %convert_element_type.15), channel_id=2, replica_groups=mesh['blk'=16,'smp'=8] {'smp'}, dimensions={0}, use_global_device_ids=true | all-gather | bytes 147456 | tf_op jit(solution)/shard_map/all_gather | solution.py:138
  405.9 2.3 fusion.18
  408.2 0.1 fusion.34
  408.3 0.1 squeeze.28
  408.4 0.1 squeeze.29
  408.5 0.1 squeeze.30
  408.5 0.1 squeeze.31
  408.6 0.1 squeeze.32
  408.7 1.0 fusion.17
  409.7 0.0 all-gather.6.cloned.1.call-update
  409.8 0.6 dynamic-slice
  411.0 1.5 copy.17
  412.5 1.6 fusion.12
  414.2 33.2 %all-gather.6.cloned.1.call-done = bf16[8,32,2048]{2,0,1:T(8,128)(2,1)} async-done(((bf16[8,2,2048]{2,0,1:T(8,128)(2,1)}), bf16[8,32,2048]{2,0,1:T(8,128)(2,1)}) %all-gather.6.cloned.1.call-update) | async-done | bytes 1048592 | tf_op jit(solution)/shard_map/all_gather | solution.py:145
  447.4 2.0 fusion.14
  449.3 0.1 maximum_multiply_fusion
  449.4 20.5 %all-reduce = f32[8,2,64]{2,1,0:T(2,128)S(1)} all-reduce(f32[8,2,64]{2,1,0:T(2,128)S(1)} %maximum_multiply_fusion), channel_id=3, replica_groups=mesh['blk'=16,'smp'=8] {'smp'}, use_global_device_ids=true, to_apply=%region_4.5.clone | all-reduce | flops 1024 | bytes 8192
  469.9 0.7 constant_dynamic-slice_fusion
  (25 shorter events, 0.2 us)
Async XLA Ops:
  8.0 11.9 %copy-start = (bf16[2048,8]{0,1:T(8,128)(2,1)S(1)}, bf16[2048,8]{0,1:T(8,128)(2,1)}, u32[]{:S(2)}) copy-start(bf16[2048,8]{0,1:T(8,128)(2,1)} %param.6) | copy-start | bytes 98308
  8.0 250.7 %all-reduce.4.cloned.1.call-start = ((), (), s32[]{:S(2)}) async-start(), calls=%async_computation.2 | async-start | bytes 10649600 | tf_op jit(solution)/shard_map/psum | solution.py:132
  8.8 11.1 %copy-start.2 = (bf16[2048,512]{1,0:T(8,128)(2,1)S(1)}, bf16[2048,512]{1,0:T(8,128)(2,1)}, u32[]{:S(2)}) copy-start(bf16[2048,512]{1,0:T(8,128)(2,1)} %param.5) | copy-start | bytes 6291460
  19.9 3.2 copy-start.4
  22.3 390.2 %all-gather.4.cloned.1.call-start = ((), (), s32[]{:S(2)}) async-start(), calls=%async_computation | async-start | bytes 1114112 | tf_op jit(solution)/shard_map/all_gather | solution.py:147
  22.9 424.5 %all-gather.6.cloned.1.call-start = ((), (), s32[]{:S(2)}) async-start(), calls=%async_computation.1 | async-start | bytes 1114112 | tf_op jit(solution)/shard_map/all_gather | solution.py:145
  258.7 4.9 %copy-start.3 = (f32[5,8,512]{2,1,0:T(8,128)S(1)}, f32[5,8,512]{2,1,0:T(8,128)}, u32[]{:S(2)}) copy-start(f32[5,8,512]{2,1,0:T(8,128)} %get-tuple-element.5) | copy-start | bytes 245764
  258.7 4.9 %copy-start.1 = (f32[2]{0:T(128)S(1)}, f32[2]{0:T(128)}, u32[]{:S(2)}) copy-start(f32[2]{0:T(128)} %lam_ref.1) | copy-start | bytes 28
  262.0 147.8 %copy-start.5 = (u32[128]{0:T(128)S(1)}, u32[128]{0:T(128)}, u32[]{:S(2)}) copy-start(u32[128]{0:T(128)} %constant.34) | copy-start | bytes 1540
Sparse Core Ops, SparseCore 0:
  22.4 236.2 all-reduce.3
Sparse Core Ops, SparseCore 1:
  24.5 72.4 all-gather.3
  409.8 37.5 all-gather.5

commit v2 on v1

v2 whole, which is shorter than its diff:
```python
import math

import jax
import jax.numpy as jnp
from jax import lax
from jax.experimental import pallas as pl
from jax.experimental.pallas import tpu as pltpu
from jax.sharding import PartitionSpec as P

HI = lax.Precision.HIGHEST
NB = 4
BLK = [(p, q) for p in range(NB) for q in range(p, NB)]
IDX = {pq: i for i, pq in enumerate(BLK)}


def lanes(x, m):
    return jnp.broadcast_to(x[:, m:m + 1], x.shape)


def subl(x, m):
    return jnp.broadcast_to(x[m:m + 1, :], x.shape)


def sweep_step(groups):
    a0 = groups[0]
    lane = lax.broadcasted_iota(jnp.int32, (8, 128), 1)
    sub = lax.broadcasted_iota(jnp.int32, (8, 128), 0)
    cols = [lanes(a0, m) for m in range(8)]
    s = {(i, m): subl(cols[m], i) for m in range(8) for i in range(m, 8)}
    z = [jnp.where(lane < 8, jnp.where(lane == m, -1.0, 0.0), subl(a0, m)) for m in range(8)]
    d, l = [None] * 8, {}
    for m in range(8):
        d[m] = 1.0 / s[m, m]
        for i in range(m + 1, 8):
            l[i, m] = s[i, m] * d[m]
        for j in range(m + 1, 8):
            for i in range(j, 8):
                s[i, j] = s[i, j] - l[i, m] * s[j, m]
        for i in range(m + 1, 8):
            z[i] = z[i] - l[i, m] * z[m]
    q = [z[m] * d[m] for m in range(8)]
    for m in range(7, -1, -1):
        for i in range(m):
            q[i] = q[i] - l[m, i] * q[m]
    out = []
    for g in range(1, 16):
        a = groups[g]
        new = jnp.where(lane < 8, 0.0, a)
        for m in range(8):
            new = new - lanes(a, m) * q[m]
        out.append(pltpu.roll(new, 120, 1))
    new = q[0]
    for m in range(1, 8):
        new = jnp.where(sub == m, q[m], new)
    out.append(pltpu.roll(new, 120, 1))
    return out


def inverse(mats):
    def body(_, carry):
        return tuple(tuple(sweep_step(list(c))) for c in carry)
    init = tuple(tuple(m[8 * g:8 * g + 8, :] for g in range(16)) for m in mats)
    out = lax.fori_loop(0, 16, body, init)
    return [-jnp.concatenate(list(c), axis=0) for c in out]


def dot(a, b, ca=1, cb=0):
    return lax.dot_general(a, b, (((ca,), (cb,)), ((), ())), precision=HI, preferred_element_type=jnp.float32)


def solve_kernel(lam_ref, a_ref, out_ref, s_ref, t_ref, y_ref, x_ref):
    n = 16384.0
    row = lax.broadcasted_iota(jnp.int32, (128, 128), 0)
    col = lax.broadcasted_iota(jnp.int32, (128, 128), 1)
    for j in range(2):
        shift = lam_ref[j] * n
        for p in range(NB):
            for q in range(p, NB):
                v = jnp.concatenate([a_ref[s, IDX[p, q]] for s in range(8)], axis=0)
                if p == q:
                    v = v + jnp.where(row == col, shift, 0.0)
                s_ref[j, p, :, 128 * q:128 * q + 128] = v
        for s in range(8):
            for q in range(NB):
                y_ref[j, s:s + 1, 128 * q:128 * q + 128] = a_ref[s, 10, q:q + 1, :]
    for p in range(NB):
        lo, hi = 128 * p, 128 * p + 128
        ws = inverse([s_ref[j, p, :, lo:hi] for j in range(2)])
        for j in range(2):
            w = ws[j]
            y = dot(y_ref[j, :, lo:hi], w)
            y_ref[j, :, lo:hi] = y
            if p + 1 < NB:
                right = s_ref[j, p, :, hi:]
                t = dot(w, right)
                t_ref[j, p, :, hi:] = t
                y_ref[j, :, hi:] = y_ref[j, :, hi:] - dot(y, right)
                for q in range(p + 1, NB):
                    k = 128 * q
                    s_ref[j, q, :, k:] = s_ref[j, q, :, k:] - dot(s_ref[j, p, :, k:k + 128], t_ref[j, p, :, k:], 0, 0)
    for j in range(2):
        for p in range(NB - 2, -1, -1):
            lo, hi = 128 * p, 128 * p + 128
            y_ref[j, :, lo:hi] = y_ref[j, :, lo:hi] - dot(y_ref[j, :, hi:], t_ref[j, p, :, hi:], 1, 1)
    for t in range(8):
        for j in range(2):
            x_ref[2 * t + j:2 * t + j + 1, :] = y_ref[j, t:t + 1, :]
    out_ref[...] = x_ref[...].astype(jnp.bfloat16)


def solve(lam, a):
    return pl.pallas_call(
        solve_kernel,
        out_shape=jax.ShapeDtypeStruct((16, 512), jnp.bfloat16),
        in_specs=[pl.BlockSpec(memory_space=pltpu.SMEM), pl.BlockSpec(memory_space=pltpu.VMEM)],
        out_specs=pl.BlockSpec(memory_space=pltpu.VMEM),
        scratch_shapes=[pltpu.VMEM((2, 4, 128, 512), jnp.float32), pltpu.VMEM((2, 4, 128, 512), jnp.float32), pltpu.VMEM((2, 8, 512), jnp.float32), pltpu.VMEM((16, 512), jnp.float32)],
        compiler_params=pltpu.CompilerParams(vmem_limit_bytes=40 << 20),
    )(lam, a)


MESH = pl.DeviceIdType.MESH
FOLDS = 5
BLOCK = 512
TRAITS = 8
SLOTS = 11


def to_smp(device):
    return {"smp": device}


def gram_kernel(x_ref, yt_ref, fold_ref, out_ref, lhs, part, relay, plain, comb, half, zin, done, send, recv, gsend, grecv):
    me = lax.axis_index("smp")
    y, z = lax.div(me, 2), lax.rem(me, 2)
    right = lax.rem(y + 1, 4) * 2 + z
    left = lax.rem(y + 3, 4) * 2 + z
    across = lax.rem(y + 2, 4)
    other = y * 2 + (1 - z)
    barrier = pltpu.get_barrier_semaphore()

    def greet(i, carry):
        pl.semaphore_signal(barrier, inc=1, device_id=to_smp(lax.rem(me + i, 8)), device_id_type=MESH)
        return carry

    lax.fori_loop(1, 8, greet, 0)

    @pl.when(me >= FOLDS)
    def _():
        out_ref[...] = jnp.zeros_like(out_ref)

    lhs[0:256, :] = jnp.transpose(x_ref[:, 0:256])
    lhs[256:272, :] = yt_ref[...]
    lhs[272:528, :] = jnp.transpose(x_ref[:, 256:512])

    def hop(kind, k, src, dst, device):
        return pltpu.make_async_remote_copy(
            src_ref=src, dst_ref=dst, send_sem=send.at[kind, k], recv_sem=recv.at[kind, k],
            device_id=to_smp(device), device_id_type=MESH)

    def relays(k):
        return [hop(0, k, part.at[across * 2, k], relay.at[0, k], right),
                hop(1, k, part.at[across * 2 + 1, k], relay.at[1, k], left)]

    def plains(k):
        return [hop(2, k, part.at[lax.rem(y + 1, 4) * 2 + 1, k], plain.at[0, k], right),
                hop(3, k, part.at[lax.rem(y + 3, 4) * 2, k], plain.at[1, k], left)]

    def combs(k):
        return [hop(4, k, relay.at[0, k], comb.at[0, k], right),
                hop(5, k, relay.at[1, k], comb.at[1, k], left)]

    def cross_z(k):
        return hop(6, k, half.at[k], zin.at[k], other)

    def gather(k):
        return pltpu.make_async_remote_copy(
            src_ref=done.at[k], dst_ref=out_ref.at[me], send_sem=gsend.at[k], recv_sem=grecv.at[me],
            device_id=to_smp(k), device_id_type=MESH)

    def products(k):
        mask = jnp.where(fold_ref[...] != k, 1.0, 0.0).astype(jnp.bfloat16)
        top = jnp.dot(lhs[0:272, :] * mask, x_ref[...], preferred_element_type=jnp.float32)
        low = jnp.dot(lhs[272:528, :] * mask, x_ref[:, 256:512], preferred_element_type=jnp.float32)
        for s in range(8):
            slot = 0
            for p in range(4):
                for q in range(p, 4):
                    r = 128 * p + 16 * s
                    if p < 2:
                        v = top[r:r + 16, 128 * q:128 * q + 128]
                    else:
                        v = low[r - 256:r - 240, 128 * q - 256:128 * q - 128]
                    part[s, k, slot] = v
                    slot += 1
            for q in range(4):
                part[s, k, slot, q:q + 1, :] = top[256 + s:257 + s, 128 * q:128 * q + 128]
            part[s, k, slot, 4:16, :] = jnp.zeros((12, 128), jnp.float32)

    def step(i, carry):
        @pl.when(i < FOLDS)
        def _():
            products(i)

            @pl.when(i == 0)
            def _():
                pl.semaphore_wait(barrier, 7)

            for c in relays(i):
                c.start()
            for c in plains(i):
                c.start()

        @pl.when((i >= 1) & (i < 1 + FOLDS))
        def _():
            k = i - 1
            for c in relays(k):
                c.wait_recv()
            relay[0, k] += part[lax.rem(y + 1, 4) * 2, k]
            relay[1, k] += part[lax.rem(y + 3, 4) * 2 + 1, k]
            for c in combs(k):
                c.start()

        @pl.when((i >= 3) & (i < 3 + FOLDS))
        def _():
            k = i - 3
            for c in plains(k) + combs(k):
                c.wait_recv()
            zero = part[y * 2, k] + plain[1, k] + comb[0, k]
            one = part[y * 2 + 1, k] + plain[0, k] + comb[1, k]
            half[k] = jnp.where(z == 0, one, zero)
            done[k] = jnp.where(z == 0, zero, one)
            cross_z(k).start()

        @pl.when(i >= 5)
        def _():
            k = i - 5
            cross_z(k).wait_recv()
            done[k] += zin[k]

            @pl.when(me != k)
            def _():
                gather(k).start()

            @pl.when(me == k)
            def _():
                out_ref[me] = done[k]

        return carry

    lax.fori_loop(0, 5 + FOLDS, step, 0)

    def finish(k, carry):
        for c in relays(k) + plains(k) + combs(k):
            c.wait_send()
        cross_z(k).wait_send()

        @pl.when(me != k)
        def _():
            gather(k).wait_send()

        return carry

    lax.fori_loop(0, FOLDS, finish, 0)

    @pl.when(me < FOLDS)
    def _():
        def arrive(i, carry):
            s = lax.rem(me + i, 8)
            pltpu.make_async_remote_copy(
                src_ref=done.at[0], dst_ref=out_ref.at[s], send_sem=gsend.at[0], recv_sem=grecv.at[s],
                device_id=to_smp(s), device_id_type=MESH).wait_recv()
            return carry

        lax.fori_loop(1, 8, arrive, 0)


def gram_sums(x, yt, fold):
    piece = (SLOTS, 16, 128)
    vmem = pl.BlockSpec(memory_space=pltpu.VMEM)
    f32 = jnp.float32
    return pl.pallas_call(
        gram_kernel,
        out_shape=jax.ShapeDtypeStruct((8,) + piece, f32),
        in_specs=[vmem] * 3,
        out_specs=vmem,
        scratch_shapes=[
            pltpu.VMEM((528, x.shape[0]), jnp.bfloat16),
            pltpu.VMEM((8, FOLDS) + piece, f32),
            pltpu.VMEM((2, FOLDS) + piece, f32),
            pltpu.VMEM((2, FOLDS) + piece, f32),
            pltpu.VMEM((2, FOLDS) + piece, f32),
            pltpu.VMEM((FOLDS,) + piece, f32),
            pltpu.VMEM((FOLDS,) + piece, f32),
            pltpu.VMEM((FOLDS,) + piece, f32),
            pltpu.SemaphoreType.DMA((7, FOLDS)),
            pltpu.SemaphoreType.DMA((7, FOLDS)),
            pltpu.SemaphoreType.DMA((FOLDS,)),
            pltpu.SemaphoreType.DMA((8,)),
        ],
        compiler_params=pltpu.CompilerParams(collective_id=1, has_side_effects=True, vmem_limit_bytes=40 << 20),
    )(x, yt, fold)


def tail_kernel(beta_ref, x_ref, fold_ref, old_ref, oof_ref, cross_ref, betas, mine, feats, terms, rows, sums,
                bsend, brecv, fsend, frecv, tsend, trecv, ssend, srecv):
    s, b = lax.axis_index("smp"), lax.axis_index("blk")
    samples = x_ref.shape[0]
    barrier = pltpu.get_barrier_semaphore()

    def greet_smp(i, carry):
        pl.semaphore_signal(barrier, inc=1, device_id={"smp": lax.rem(s + i, 8)}, device_id_type=MESH)
        return carry

    def greet_blk(i, carry):
        pl.semaphore_signal(barrier, inc=1, device_id={"blk": lax.rem(b + i, 16)}, device_id_type=MESH)
        return carry

    lax.fori_loop(1, 8, greet_smp, 0)
    lax.fori_loop(1, 16, greet_blk, 0)
    pl.semaphore_wait(barrier, 22)

    def spread(i):
        return pltpu.make_async_remote_copy(
            src_ref=beta_ref, dst_ref=betas.at[s], send_sem=bsend.at[i], recv_sem=brecv.at[s],
            device_id={"smp": lax.rem(s + i, 8)}, device_id_type=MESH)

    def start_spread(i, carry):
        spread(i).start()
        return carry

    def end_spread(i, carry):
        spread(i).wait_send()
        return carry

    @pl.when(s < FOLDS)
    def _():
        lax.fori_loop(1, 8, start_spread, 0)
        betas[s] = beta_ref[...]

    def beta_in(k, carry):
        @pl.when(s != k)
        def _():
            pltpu.make_async_remote_copy(
                src_ref=beta_ref, dst_ref=betas.at[k], send_sem=bsend.at[0], recv_sem=brecv.at[k],
                device_id={"smp": k}, device_id_type=MESH).wait_recv()
        return carry

    lax.fori_loop(0, FOLDS, beta_in, 0)
    flat = jnp.concatenate([betas[k] for k in range(FOLDS)], axis=0)
    fitted = lax.dot_general(flat, x_ref[...], (((1,), (1,)), ((), ())), preferred_element_type=jnp.float32)
    fold = fold_ref[...]
    chosen = jnp.zeros((16, samples), jnp.float32)
    for k in range(FOLDS):
        chosen = jnp.where(fold == k, fitted[16 * k:16 * k + 16, :], chosen)
    oof = (chosen * math.sqrt(8 * samples / BLOCK)).astype(jnp.bfloat16)
    oof_ref[...] = oof
    for c in range(16):
        mine[c] = oof[:, 128 * c:128 * c + 128]
    feats[b] = mine[b]

    def feature(i):
        to = lax.rem(b + i, 16)
        return pltpu.make_async_remote_copy(
            src_ref=mine.at[to], dst_ref=feats.at[b], send_sem=fsend.at[i], recv_sem=frecv.at[i],
            device_id={"blk": to}, device_id_type=MESH)

    def start_feature(i, carry):
        feature(i).start()
        return carry

    def end_feature(i, carry):
        feature(i).wait()
        return carry

    lax.fori_loop(1, 16, start_feature, 0)
    lax.fori_loop(1, 16, end_feature, 0)
    f = jnp.concatenate([feats[c] for c in range(16)], axis=0)
    nt = (((1,), (1,)), ((), ()))
    against_old = lax.dot_general(f, old_ref[...], nt, preferred_element_type=jnp.float32)
    against_new = lax.dot_general(f, f, nt, preferred_element_type=jnp.float32)
    r = lax.broadcasted_iota(jnp.int32, (256, 256), 0)
    c = lax.broadcasted_iota(jnp.int32, (256, 256), 1)
    row_trait = (r >> 1) & 7
    against_old = jnp.where(row_trait == (c >> 5), against_old, 0.0)
    against_new = jnp.where(row_trait == ((c >> 1) & 7), against_new, 0.0)
    r = lax.broadcasted_iota(jnp.int32, (256, 128), 0)
    c = lax.broadcasted_iota(jnp.int32, (256, 128), 1)
    pick_old = jnp.where((r & 31) == c, 1.0, 0.0)
    pick_new = jnp.where(32 + ((r >> 4) << 1) + (r & 1) == c, 1.0, 0.0)
    total = dot(against_old, pick_old) + dot(against_new, pick_new)
    for k in range(16):
        terms[k] = total[16 * k:16 * k + 16, :]
    rows[b] = terms[b]

    def term(i):
        to = lax.rem(b + i, 16)
        return pltpu.make_async_remote_copy(
            src_ref=terms.at[to], dst_ref=rows.at[b], send_sem=tsend.at[i], recv_sem=trecv.at[i],
            device_id={"blk": to}, device_id_type=MESH)

    def start_term(i, carry):
        term(i).start()
        return carry

    def end_term(i, carry):
        term(i).wait()
        return carry

    lax.fori_loop(1, 16, start_term, 0)
    lax.fori_loop(1, 16, end_term, 0)
    part = rows[0]
    for k in range(1, 16):
        part = part + rows[k]
    sums[s] = part

    def last(i):
        return pltpu.make_async_remote_copy(
            src_ref=sums.at[s], dst_ref=sums.at[s], send_sem=ssend.at[i], recv_sem=srecv.at[i],
            device_id={"smp": lax.rem(s + i, 8)}, device_id_type=MESH)

    def start_last(i, carry):
        last(i).start()
        return carry

    def end_last(i, carry):
        last(i).wait()
        return carry

    lax.fori_loop(1, 8, start_last, 0)
    lax.fori_loop(1, 8, end_last, 0)
    final = sums[0]
    for k in range(1, 8):
        final = final + sums[k]
    cross_ref[...] = final * (1.0 / (8 * samples))

    @pl.when(s < FOLDS)
    def _():
        lax.fori_loop(1, 8, end_spread, 0)


def tail(beta, x, fold, old):
    vmem = pl.BlockSpec(memory_space=pltpu.VMEM)
    dma = pltpu.SemaphoreType.DMA
    return pl.pallas_call(
        tail_kernel,
        out_shape=(jax.ShapeDtypeStruct((16, x.shape[0]), jnp.bfloat16), jax.ShapeDtypeStruct((16, 128), jnp.float32)),
        in_specs=[vmem] * 4,
        out_specs=(vmem, vmem),
        scratch_shapes=[
            pltpu.VMEM((FOLDS, 16, BLOCK), jnp.bfloat16),
            pltpu.VMEM((16, 16, 128), jnp.bfloat16),
            pltpu.VMEM((16, 16, 128), jnp.bfloat16),
            pltpu.VMEM((16, 16, 128), jnp.float32),
            pltpu.VMEM((16, 16, 128), jnp.float32),
            pltpu.VMEM((8, 16, 128), jnp.float32),
            dma((8,)), dma((8,)), dma((16,)), dma((16,)), dma((16,)), dma((16,)), dma((8,)), dma((8,)),
        ],
        compiler_params=pltpu.CompilerParams(collective_id=2, has_side_effects=True, vmem_limit_bytes=40 << 20),
    )(beta, x, fold, old)


def local(x, y, fold, lam, old):
    rows = x.shape[0]
    fold = fold[None, :]
    yt = jnp.pad(y.T, ((0, 8), (0, 0)))
    pieces = gram_sums(x, yt, fold)
    beta = solve(lam, pieces)
    before = jnp.transpose(old[0], (1, 2, 0)).reshape(256, 128)
    oof, cross = tail(beta, x, fold, before)
    here = lax.dynamic_slice_in_dim(cross, 8 * lax.axis_index("smp"), 8, 1)
    return jnp.transpose(oof.reshape(TRAITS, 2, rows), (2, 0, 1)), here.reshape(TRAITS, 2, 8)


def solution(mesh):
    return jax.shard_map(
        local,
        mesh=mesh,
        in_specs=(P("smp", "blk"), P("smp", None), P("smp"), P(), P("smp", "blk", None, None)),
        out_specs=(P("smp", None, "blk"), P(None, "blk", "smp")),
        check_vma=False,
    )
```

time: 481 us -> 197 us (0.41)
  waiting for transfers between devices: 269 us -> 0 us
  Pallas kernels: 113 us -> 192 us
  blocking collectives: 50 us -> 0 us
  matrix products: 19.4 us -> 0 us
  between operations: 16.4 us -> 0.7 us
  other arithmetic: 6.56 us -> 0 us
    psum x1 -> x0, waiting for transfers between devices: 236 us -> none  [local(): gram, xy = lax.psum((gram, xy), 'smp')]
    pallas_call x0 -> x2, Pallas kernels: none -> 79.4 us  [the longest x1 49.7 us: gram_sums(): pl.pallas_call(gram_kernel, out_shape=jax.ShapeDtypeStruct((8,) + piece,...]
    all_gather x2 -> x0, waiting for transfers between devices: 33.2 us -> none  [the longest x1 33.2 us: local(): everyone = lax.all_gather(oof, 'blk', axis=1, tiled=True)]
    all_gather x1 -> x0, blocking collectives: 29.5 us -> none  [local(): lax.all_gather(beta, 'smp', axis=0)[:FOLDS].reshape(FOLDS * 16, BLOCK)]
    unnamed x1 -> x0, blocking collectives: 20.5 us -> none
    dot_general x5 -> x0, matrix products: 19.4 us -> none  [the longest x1 11.1 us: local(): jnp.einsum('rpe,ro->peo', masked, x, preferred_element_type=jnp.float32)]
  transfers between devices with their start and end apart: 3 -> 0, of which waited for: 2 -> 0; matrix products, arithmetic and copies ran while one was open for 3% -> 0% of each run, Pallas kernels for 24% -> 0%
where the time goes in v2:
time: 197 us
  Pallas kernels  192 us (97%)
  local copies, waits for them, and re-layouts  4.45 us (2%)
    pallas_call x1, Pallas kernels, solve(): pl.pallas_call(solve_kernel, out_shape=jax.ShapeDtypeStruct((16, 512), jn...  113 us
    pallas_call x1, Pallas kernels, gram_sums(): pl.pallas_call(gram_kernel, out_shape=jax.ShapeDtypeStruct((8,) + piece,...  49.7 us
    pallas_call x1, Pallas kernels, tail(): pl.pallas_call(tail_kernel, out_shape=(jax.ShapeDtypeStruct((16, x.shape[...  29.7 us

profile of v2, /device:TPU:1, one launch (start us, length us, event | category | flops | bytes accessed | tf_op | source)
XLA Modules:
  0.0 197.3 jit_solution(7717016703783756674)
XLA Ops:
  0.6 0.0 copy-start.4
  0.6 0.0 copy-start.2
  0.7 0.8 pad.4.yt_ref
  1.4 0.0 copy-start
  1.4 1.6 copy-done
  3.0 0.0 copy-start.3
  3.0 0.7 copy-done.3
  3.7 0.0 copy-start.1
  3.7 49.7 %shard_map.68.a_ref = f32[8,11,16,128]{3,2,1,0:T(8,128)S(1)} custom-call(bf16[2048,512]{1,0:T(8,128)(2,1)S(1)} %copy-done, bf16[16,2048]{1,0:T(8,128)(2,1)S(1)} %pad.4.yt_ref, s32[1,2048]{1,0:T(1,128)S(1)} %bitcast.10), custom_call_target="tpu_custom_call" | custom-call | tf_op jit(solution)/shard_map/pallas_call | solution.py:282
  53.4 0.0 copy-done.4
  53.4 112.7 %shard_map.69.beta_ref = bf16[16,512]{1,0:T(8,128)(2,1)S(1)} custom-call(f32[2]{0:T(128)S(1)} %copy-done.4, f32[8,11,16,128]{3,2,1,0:T(8,128)S(1)} %shard_map.68.a_ref), custom_call_target="tpu_custom_call" | custom-call | tf_op jit(solution)/shard_map/pallas_call | solution.py:112
  166.1 0.0 copy-done.2
  166.2 0.0 copy-done.1
  166.2 29.7 %shard_map.70 = (bf16[16,2048]{1,0:T(8,128)(2,1)S(1)}, f32[16,128]{1,0:T(8,128)S(1)}) custom-call(bf16[16,512]{1,0:T(8,128)(2,1)S(1)} %shard_map.69.beta_ref, bf16[2048,512]{1,0:T(8,128)(2,1)S(1)} %copy-done.1, s32[1,2048]{1,0:T(1,128)S(1)} %bitcast.11, bf16[256,128]{1,0:T(8,128)(2,1)S(1)} %bitcast.9), custom_call_target="tpu_custom_call" | custom-call | tf_op jit(solution)/shard_map/pallas_call | solution.py:445
  195.9 0.7 reshape.14
  196.6 0.7 constant_dynamic-slice_fusion
Async XLA Ops:
  0.6 52.8 %copy-start.4 = (f32[2]{0:T(128)S(1)}, f32[2]{0:T(128)}, u32[]{:S(2)}) copy-start(f32[2]{0:T(128)} %lam_ref.1) | copy-start | bytes 28
  0.6 165.5 %copy-start.2 = (bf16[1,128,8,32]{1,3,2,0:T(8,128)(2,1)S(1)}, bf16[1,128,8,32]{1,3,2,0:T(8,128)(2,1)}, u32[]{:S(2)}) copy-start(bf16[1,128,8,32]{1,3,2,0:T(8,128)(2,1)} %param.9) | copy-start | bytes 196612
  1.4 1.6 copy-start
  3.0 0.7 copy-start.3
  3.7 162.4 %copy-start.1 = (bf16[2048,512]{1,0:T(8,128)(2,1)S(1)}, bf16[2048,512]{1,0:T(8,128)(2,1)}, u32[]{:S(2)}) copy-start(bf16[2048,512]{1,0:T(8,128)(2,1)} %x_ref.3) | copy-start | bytes 6291460

commit v3 on v2

--- a/solution.py
+++ b/solution.py
@@ -21,47 +21,61 @@
     return jnp.broadcast_to(x[m:m + 1, :], x.shape)
 
 
-def sweep_step(groups):
-    a0 = groups[0]
+def split3(x):
+    hi = x.astype(jnp.bfloat16).astype(jnp.float32)
+    r = x - hi
+    mid = r.astype(jnp.bfloat16).astype(jnp.float32)
+    return hi, mid, r - mid
+
+
+def pivots(a0, base, lane, sub):
+    cols = [lanes(a0, base + m) for m in range(8)]
+    inside = (lane >= base) & (lane < base + 8)
+    z = jnp.where(inside, jnp.where(lane - base == sub, -1.0, 0.0), a0)
+    scale = None
+    for m in range(8):
+        d = 1.0 / subl(cols[m], m)
+        l = jnp.where(sub == m, 0.0, cols[m] * d)
+        z = z - l * subl(z, m)
+        for j in range(m + 1, 8):
+            cols[j] = cols[j] - l * subl(cols[j], m)
+        scale = d if m == 0 else jnp.where(sub == m, d, scale)
+    return z * scale, inside
+
+
+def inverse(mats):
+    n = len(mats)
     lane = lax.broadcasted_iota(jnp.int32, (8, 128), 1)
     sub = lax.broadcasted_iota(jnp.int32, (8, 128), 0)
-    cols = [lanes(a0, m) for m in range(8)]
-    s = {(i, m): subl(cols[m], i) for m in range(8) for i in range(m, 8)}
-    z = [jnp.where(lane < 8, jnp.where(lane == m, -1.0, 0.0), subl(a0, m)) for m in range(8)]
-    d, l = [None] * 8, {}
-    for m in range(8):
-        d[m] = 1.0 / s[m, m]
-        for i in range(m + 1, 8):
-            l[i, m] = s[i, m] * d[m]
-        for j in range(m + 1, 8):
-            for i in range(j, 8):
-                s[i, j] = s[i, j] - l[i, m] * s[j, m]
-        for i in range(m + 1, 8):
-            z[i] = z[i] - l[i, m] * z[m]
-    q = [z[m] * d[m] for m in range(8)]
-    for m in range(7, -1, -1):
-        for i in range(m):
-            q[i] = q[i] - l[m, i] * q[m]
-    out = []
-    for g in range(1, 16):
-        a = groups[g]
-        new = jnp.where(lane < 8, 0.0, a)
-        for m in range(8):
-            new = new - lanes(a, m) * q[m]
-        out.append(pltpu.roll(new, 120, 1))
-    new = q[0]
-    for m in range(1, 8):
-        new = jnp.where(sub == m, q[m], new)
-    out.append(pltpu.roll(new, 120, 1))
-    return out
-
-
-def inverse(mats):
-    def body(_, carry):
-        return tuple(tuple(sweep_step(list(c))) for c in carry)
-    init = tuple(tuple(m[8 * g:8 * g + 8, :] for g in range(16)) for m in mats)
-    out = lax.fori_loop(0, 16, body, init)
-    return [-jnp.concatenate(list(c), axis=0) for c in out]
+    mats = [[a[8*i:8*i+8] for i in range(16)] for a in mats]
+    for g in range(16):
+        for t in range(n):
+            a = mats[t]
+            base = 8 * g
+            a0 = a[g]
+            qs, inside = pivots(a0, base, lane, sub)
+            h, m, l = split3(a0)
+            lhs = jnp.concatenate([h, h, m, h, l, m], axis=0).astype(jnp.bfloat16)
+            h, m, l = split3(qs)
+            rhs = jnp.concatenate([h, m, h, l, h, m], axis=0).astype(jnp.bfloat16)
+            upd = lax.dot_general(lhs, rhs, (((0,), (0,)), ((), ())), preferred_element_type=jnp.float32)
+            new = []
+            for i in range(16):
+                if i == g:
+                    v = qs
+                elif i == g + 1:
+                    v = jnp.where(inside, 0.0, a[i])
+                    t1 = v - lanes(a[i], base) * subl(qs, 0)
+                    t2 = lanes(a[i], base + 1) * subl(qs, 1)
+                    for m in range(2, 8, 2):
+                        t1 = t1 - lanes(a[i], base + m) * subl(qs, m)
+                        t2 = t2 + lanes(a[i], base + m + 1) * subl(qs, m + 1)
+                    v = t1 - t2
+                else:
+                    v = jnp.where(inside, 0.0, a[i]) - upd[8*i:8*i+8]
+                new.append(v)
+            mats[t] = new
+    return [-jnp.concatenate(a, axis=0) for a in mats]
 
 
 def dot(a, b, ca=1, cb=0):

time: 197 us -> 107 us (0.54)
  Pallas kernels: 192 us -> 101 us
    pallas_call x1, Pallas kernels: 113 us -> 22 us  [solve(): pl.pallas_call(solve_kernel, out_shape=jax.ShapeDtypeStruct((16, 512), jn...]
where the time goes in v3:
time: 107 us
  Pallas kernels  101 us (94%)
  local copies, waits for them, and re-layouts  4.45 us (4%)
    pallas_call x1, Pallas kernels, gram_sums(): pl.pallas_call(gram_kernel, out_shape=jax.ShapeDtypeStruct((8,) + piece,...  49.7 us
    pallas_call x1, Pallas kernels, tail(): pl.pallas_call(tail_kernel, out_shape=(jax.ShapeDtypeStruct((16, x.shape[...  29.7 us
    pallas_call x1, Pallas kernels, solve(): pl.pallas_call(solve_kernel, out_shape=jax.ShapeDtypeStruct((16, 512), jn...  22 us
    unnamed x10, local copies, waits for them, and re-layouts  2.3 us

profile of v3, /device:TPU:1, one launch (start us, length us, event | category | flops | bytes accessed | tf_op | source)
XLA Modules:
  0.0 106.6 jit_solution(9491193523250000414)
XLA Ops:
  0.6 0.0 copy-start.4
  0.6 0.0 copy-start.2
  0.7 0.8 pad.4.yt_ref
  1.4 0.0 copy-start
  1.4 1.6 %copy-done = bf16[2048,512]{1,0:T(8,128)(2,1)S(1)} copy-done((bf16[2048,512]{1,0:T(8,128)(2,1)S(1)}, bf16[2048,512]{1,0:T(8,128)(2,1)}, u32[]{:S(2)}) %copy-start) | copy-done | bytes 2097176
  3.0 0.0 copy-start.3
  3.0 0.7 copy-done.3
  3.7 0.0 copy-start.1
  3.7 49.7 %shard_map.68.a_ref = f32[8,11,16,128]{3,2,1,0:T(8,128)S(1)} custom-call(bf16[2048,512]{1,0:T(8,128)(2,1)S(1)} %copy-done, bf16[16,2048]{1,0:T(8,128)(2,1)S(1)} %pad.4.yt_ref, s32[1,2048]{1,0:T(1,128)S(1)} %bitcast.10), custom_call_target="tpu_custom_call" | custom-call | tf_op jit(solution)/shard_map/pallas_call | solution.py:296
  53.4 0.0 copy-done.4
  53.4 22.0 %shard_map.69.beta_ref = bf16[16,512]{1,0:T(8,128)(2,1)S(1)} custom-call(f32[2]{0:T(128)S(1)} %copy-done.4, f32[8,11,16,128]{3,2,1,0:T(8,128)S(1)} %shard_map.68.a_ref), custom_call_target="tpu_custom_call" | custom-call | tf_op jit(solution)/shard_map/pallas_call | solution.py:126
  75.5 0.0 copy-done.2
  75.5 0.0 copy-done.1
  75.5 29.7 %shard_map.70 = (bf16[16,2048]{1,0:T(8,128)(2,1)S(1)}, f32[16,128]{1,0:T(8,128)S(1)}) custom-call(bf16[16,512]{1,0:T(8,128)(2,1)S(1)} %shard_map.69.beta_ref, bf16[2048,512]{1,0:T(8,128)(2,1)S(1)} %copy-done.1, s32[1,2048]{1,0:T(1,128)S(1)} %bitcast.11, bf16[256,128]{1,0:T(8,128)(2,1)S(1)} %bitcast.9), custom_call_target="tpu_custom_call" | custom-call | tf_op jit(solution)/shard_map/pallas_call | solution.py:459
  105.3 0.7 reshape.14
  105.9 0.7 constant_dynamic-slice_fusion
Async XLA Ops:
  0.6 52.8 %copy-start.4 = (f32[2]{0:T(128)S(1)}, f32[2]{0:T(128)}, u32[]{:S(2)}) copy-start(f32[2]{0:T(128)} %lam_ref.1) | copy-start | bytes 28
  0.6 74.9 %copy-start.2 = (bf16[1,128,8,32]{1,3,2,0:T(8,128)(2,1)S(1)}, bf16[1,128,8,32]{1,3,2,0:T(8,128)(2,1)}, u32[]{:S(2)}) copy-start(bf16[1,128,8,32]{1,3,2,0:T(8,128)(2,1)} %param.9) | copy-start | bytes 196612
  1.4 1.6 %copy-start = (bf16[2048,512]{1,0:T(8,128)(2,1)S(1)}, bf16[2048,512]{1,0:T(8,128)(2,1)}, u32[]{:S(2)}) copy-start(bf16[2048,512]{1,0:T(8,128)(2,1)} %x_ref.3) | copy-start | bytes 6291460
  3.0 0.7 copy-start.3
  3.7 71.8 %copy-start.1 = (bf16[2048,512]{1,0:T(8,128)(2,1)S(1)}, bf16[2048,512]{1,0:T(8,128)(2,1)}, u32[]{:S(2)}) copy-start(bf16[2048,512]{1,0:T(8,128)(2,1)} %x_ref.3) | copy-start | bytes 6291460

commit v4 on v3

v4 whole, which is shorter than its diff:
```python
import math

import jax
import jax.numpy as jnp
from jax import lax
from jax.experimental import pallas as pl
from jax.experimental.pallas import tpu as pltpu
from jax.sharding import PartitionSpec as P

HI = lax.Precision.HIGHEST
NB = 4
BLK = [(p, q) for p in range(NB) for q in range(p, NB)]
IDX = {pq: i for i, pq in enumerate(BLK)}


def lanes(x, m):
    return jnp.broadcast_to(x[:, m:m + 1], x.shape)


def subl(x, m):
    return jnp.broadcast_to(x[m:m + 1, :], x.shape)


def split3(x):
    hi = x.astype(jnp.bfloat16).astype(jnp.float32)
    r = x - hi
    mid = r.astype(jnp.bfloat16).astype(jnp.float32)
    return hi, mid, r - mid


def pivots(a0, base, lane, sub):
    cols = [lanes(a0, base + m) for m in range(8)]
    inside = (lane >= base) & (lane < base + 8)
    z = jnp.where(inside, jnp.where(lane - base == sub, -1.0, 0.0), a0)
    scale = None
    for m in range(8):
        d = 1.0 / subl(cols[m], m)
        l = jnp.where(sub == m, 0.0, cols[m] * d)
        z = z - l * subl(z, m)
        for j in range(m + 1, 8):
            cols[j] = cols[j] - l * subl(cols[j], m)
        scale = d if m == 0 else jnp.where(sub == m, d, scale)
    return z * scale, inside


def inverse(mats):
    n = len(mats)
    lane = lax.broadcasted_iota(jnp.int32, (8, 128), 1)
    sub = lax.broadcasted_iota(jnp.int32, (8, 128), 0)
    mats = [[a[8 * i:8 * i + 8] for i in range(16)] for a in mats]
    for g in range(16):
        for t in range(n):
            a = mats[t]
            base = 8 * g
            a0 = a[g]
            qs, inside = pivots(a0, base, lane, sub)
            h, m, l = split3(a0)
            lhs = jnp.concatenate([h, h, m, h, l, m], axis=0).astype(jnp.bfloat16)
            h, m, l = split3(qs)
            rhs = jnp.concatenate([h, m, h, l, h, m], axis=0).astype(jnp.bfloat16)
            upd = lax.dot_general(lhs, rhs, (((0,), (0,)), ((), ())), preferred_element_type=jnp.float32)
            new = []
            for i in range(16):
                if i == g:
                    v = qs
                elif i == g + 1:
                    v = jnp.where(inside, 0.0, a[i])
                    t1 = v - lanes(a[i], base) * subl(qs, 0)
                    t2 = lanes(a[i], base + 1) * subl(qs, 1)
                    for m in range(2, 8, 2):
                        t1 = t1 - lanes(a[i], base + m) * subl(qs, m)
                        t2 = t2 + lanes(a[i], base + m + 1) * subl(qs, m + 1)
                    v = t1 - t2
                else:
                    v = jnp.where(inside, 0.0, a[i]) - upd[8 * i:8 * i + 8]
                new.append(v)
            mats[t] = new
        yield None
    yield [-jnp.concatenate(a, axis=0) for a in mats]


def dot(a, b, ca=1, cb=0):
    return lax.dot_general(a, b, (((ca,), (cb,)), ((), ())), precision=HI, preferred_element_type=jnp.float32)


MESH = pl.DeviceIdType.MESH
FOLDS = 5
BLOCK = 512
TRAITS = 8
CHUNKS = [[0, 1], [2, 3], [4, 5], [6, 7], [8], [9]]
XY_CHUNK = 1
FIRST = 4
STEPS = len(CHUNKS)
ROWS = [16 * len(c) + (8 if i == XY_CHUNK else 0) for i, c in enumerate(CHUNKS)]
START = [sum(ROWS[:i]) for i in range(STEPS)]
TOTAL = sum(ROWS)
PLACE = {slot: START[i] + 16 * n for i, c in enumerate(CHUNKS) for n, slot in enumerate(c)}
XY_PLACE = START[XY_CHUNK] + 16 * len(CHUNKS[XY_CHUNK])


def fit_kernel(lam_ref, x_ref, yt_ref, fold_ref, beta_ref, out_ref, s_ref, t_ref, y_ref, b_ref, xv, lhs, part, relay, plain, comb, half, zin, done,
                load, send, recv, gsend, grecv):
    me = lax.axis_index("smp")
    y, z = lax.div(me, 2), lax.rem(me, 2)
    right = lax.rem(y + 1, 4) * 2 + z
    left = lax.rem(y + 3, 4) * 2 + z
    across = lax.rem(y + 2, 4)
    other = y * 2 + (1 - z)
    barrier = pltpu.get_barrier_semaphore()
    loads = [pltpu.make_async_copy(x_ref.at[:, pl.ds(128 * p, 128)], xv.at[:, pl.ds(128 * p, 128)], load.at[p])
             for p in range(NB)]
    for c in loads:
        c.start()
    for i in range(1, 8):
        pl.semaphore_signal(barrier, inc=1, device_id={"smp": lax.rem(me + i, 8)}, device_id_type=MESH)

    @pl.when(me >= FOLDS)
    def _():
        out_ref[...] = jnp.zeros_like(out_ref)

    masks = [jnp.where(fold_ref[...] != k, 1.0, 0.0).astype(jnp.bfloat16) for k in range(FOLDS)]
    ready = set()

    def span(c):
        return pl.ds(FOLDS * START[c], FOLDS * ROWS[c])

    def hop(kind, c, src, dst, device):
        return pltpu.make_async_remote_copy(
            src_ref=src, dst_ref=dst, send_sem=send.at[kind, c], recv_sem=recv.at[kind, c],
            device_id={"smp": device}, device_id_type=MESH)

    def relays(c):
        return [hop(0, c, part.at[across * 2, span(c)], relay.at[0, span(c)], right),
                hop(1, c, part.at[across * 2 + 1, span(c)], relay.at[1, span(c)], left)]

    def plains(c):
        return [hop(2, c, part.at[lax.rem(y + 1, 4) * 2 + 1, span(c)], plain.at[0, span(c)], right),
                hop(3, c, part.at[lax.rem(y + 3, 4) * 2, span(c)], plain.at[1, span(c)], left)]

    def combs(c):
        return [hop(4, c, relay.at[0, span(c)], comb.at[0, span(c)], right),
                hop(5, c, relay.at[1, span(c)], comb.at[1, span(c)], left)]

    def cross_z(c):
        return hop(6, c, half.at[span(c)], zin.at[span(c)], other)

    def gather(c, k, sender):
        return pltpu.make_async_remote_copy(
            src_ref=done.at[pl.ds(FOLDS * START[c] + k * ROWS[c], ROWS[c])],
            dst_ref=out_ref.at[sender, pl.ds(START[c], ROWS[c])],
            send_sem=gsend.at[c, k], recv_sem=grecv.at[c, sender], device_id={"smp": k}, device_id_type=MESH)

    def rows_of(p):
        if p in ready:
            return
        ready.add(p)
        loads[p].wait()
        xt = jnp.transpose(xv[:, 128 * p:128 * p + 128])
        for k in range(FOLDS):
            lhs[p, 128 * k:128 * k + 128, :] = xt * masks[k]

    def products(c):
        slots = CHUNKS[c]
        p, q = BLK[slots[0]]
        wide = len(slots) == 2 and BLK[slots[1]] == (p, q + 1)
        for n, slot in enumerate(slots):
            p, q = BLK[slot]
            rows_of(p)
            if q not in ready:
                rows_of(q)
            if wide and n == 0:
                rows_of(q + 1)
                both = jnp.dot(lhs[p], xv[:, 128 * q:128 * q + 256], preferred_element_type=jnp.float32)
            v = both[:, 128 * n:128 * n + 128] if wide else jnp.dot(
                lhs[p], xv[:, 128 * q:128 * q + 128], preferred_element_type=jnp.float32)
            for k in range(FOLDS):
                for s in range(8):
                    r = FOLDS * START[c] + k * ROWS[c] + 16 * n
                    part[s, r:r + 16, :] = v[128 * k + 16 * s:128 * k + 16 * s + 16, :]
        if c == XY_CHUNK:
            for p in range(NB):
                rows_of(p)
            yt = yt_ref[...]
            v = jnp.dot(jnp.concatenate([yt * m for m in masks], axis=0), xv[...], preferred_element_type=jnp.float32)
            for k in range(FOLDS):
                r = FOLDS * START[c] + (k + 1) * ROWS[c] - 8
                for s in range(8):
                    for q in range(NB):
                        part[s, r + q:r + q + 1, :] = v[16 * k + s:16 * k + s + 1, 128 * q:128 * q + 128]
                    part[s, r + 4:r + 8, :] = jnp.zeros((4, 128), jnp.float32)

    def arrived(g):
        @pl.when(me < FOLDS)
        def _():
            def one(i, carry):
                gather(g, 0, lax.rem(me + i, 8)).wait_recv()
                return carry

            lax.fori_loop(1, 8, one, 0)

        row = lax.broadcasted_iota(jnp.int32, (128, 128), 0)
        col = lax.broadcasted_iota(jnp.int32, (128, 128), 1)
        for slot in CHUNKS[g]:
            p, q = BLK[slot]
            r = PLACE[slot]
            v = jnp.concatenate([out_ref[s, r:r + 16, :] for s in range(8)], axis=0)
            for j in range(2):
                w = v if p < q else v + jnp.where(row == col, lam_ref[j] * float(8 * x_ref.shape[0]), 0.0)
                s_ref[j, p, :, 128 * q:128 * q + 128] = w
        if g == XY_CHUNK:
            for s in range(8):
                for q in range(NB):
                    for j in range(2):
                        y_ref[j, s:s + 1, 128 * q:128 * q + 128] = out_ref[s, XY_PLACE + q:XY_PLACE + q + 1, :]

    def subtract(p, q):
        for j in range(2):
            a = s_ref[j, p, :, 128 * q:128 * q + 128]
            s_ref[j, q, :, 128 * q:] = s_ref[j, q, :, 128 * q:] - dot(a, t_ref[j, p, :, 128 * q:], 0, 0)

    def tasks():
        arrived(0)
        for p in range(NB):
            lo, hi = 128 * p, 128 * p + 128
            for n, ws in enumerate(inverse([s_ref[j, p, :, lo:hi] for j in range(2)])):
                if n % 8 == 7:
                    yield None
            if p == 0:
                arrived(1)
            for j in range(2):
                y = dot(y_ref[j, :, lo:hi], ws[j])
                y_ref[j, :, lo:hi] = y
                if p + 1 < NB:
                    right = s_ref[j, p, :, hi:]
                    t_ref[j, p, :, hi:] = dot(ws[j], right)
                    y_ref[j, :, hi:] = y_ref[j, :, hi:] - dot(y, right)
            if p == 0:
                yield None
                arrived(2)
                arrived(3)
                subtract(0, 1)
                yield None
            elif p == 1:
                arrived(4)
                arrived(5)
                for q in range(2, NB):
                    subtract(0, q)
                    subtract(1, q)
            elif p == 2:
                subtract(2, 3)
        for p in range(NB - 2, -1, -1):
            lo, hi = 128 * p, 128 * p + 128
            for j in range(2):
                y_ref[j, :, lo:hi] = y_ref[j, :, lo:hi] - dot(y_ref[j, :, hi:], t_ref[j, p, :, hi:], 1, 1)
        for t in range(TRAITS):
            for j in range(2):
                b_ref[2 * t + j:2 * t + j + 1, :] = y_ref[j, t:t + 1, :]
        beta_ref[...] = b_ref[...].astype(jnp.bfloat16)

    solving = tasks()

    for i in range(STEPS + 3):
        if i < STEPS:
            products(i)
            if i == 0:
                pl.semaphore_wait(barrier, 7)
            for c in relays(i) + plains(i):
                c.start()
        if 1 <= i <= STEPS:
            g = i - 1
            for c in relays(g):
                c.wait_recv()
            relay[0, span(g)] += part[lax.rem(y + 1, 4) * 2, span(g)]
            relay[1, span(g)] += part[lax.rem(y + 3, 4) * 2 + 1, span(g)]
            for c in combs(g):
                c.start()
        if 2 <= i <= STEPS + 1:
            g = i - 2
            for c in plains(g) + combs(g):
                c.wait_recv()
            zero = part[y * 2, span(g)] + plain[1, span(g)] + comb[0, span(g)]
            one = part[y * 2 + 1, span(g)] + plain[0, span(g)] + comb[1, span(g)]
            half[span(g)] = jnp.where(z == 0, one, zero)
            done[span(g)] = jnp.where(z == 0, zero, one)
            cross_z(g).start()
        if i >= 3:
            g = i - 3
            cross_z(g).wait_recv()
            done[span(g)] += zin[span(g)]
            for k in range(FOLDS):
                @pl.when(me != k)
                def _():
                    gather(g, k, me).start()

                @pl.when(me == k)
                def _():
                    r = FOLDS * START[g] + k * ROWS[g]
                    out_ref[me, START[g]:START[g] + ROWS[g], :] = done[r:r + ROWS[g], :]
        if i >= FIRST:
            next(solving)

    for _ in solving:
        pass
    for g in range(STEPS):
        for c in relays(g) + plains(g) + combs(g) + [cross_z(g)]:
            c.wait_send()
        for k in range(FOLDS):
            @pl.when(me != k)
            def _():
                gather(g, k, me).wait_send()


def fit(lam, x, yt, fold):
    vmem = pl.BlockSpec(memory_space=pltpu.VMEM)
    f32 = jnp.float32
    rows = FOLDS * TOTAL
    return pl.pallas_call(
        fit_kernel,
        out_shape=jax.ShapeDtypeStruct((16, BLOCK), jnp.bfloat16),
        in_specs=[pl.BlockSpec(memory_space=pltpu.SMEM), pl.BlockSpec(memory_space=pltpu.HBM), vmem, vmem],
        out_specs=vmem,
        scratch_shapes=[
            pltpu.VMEM((8, TOTAL, 128), f32),
            pltpu.VMEM((2, NB, 128, BLOCK), f32),
            pltpu.VMEM((2, NB, 128, BLOCK), f32),
            pltpu.VMEM((2, TRAITS, BLOCK), f32),
            pltpu.VMEM((16, BLOCK), f32),
            pltpu.VMEM(x.shape, jnp.bfloat16),
            pltpu.VMEM((NB, 128 * FOLDS, x.shape[0]), jnp.bfloat16),
            pltpu.VMEM((8, rows, 128), f32),
            pltpu.VMEM((2, rows, 128), f32),
            pltpu.VMEM((2, rows, 128), f32),
            pltpu.VMEM((2, rows, 128), f32),
            pltpu.VMEM((rows, 128), f32),
            pltpu.VMEM((rows, 128), f32),
            pltpu.VMEM((rows, 128), f32),
            pltpu.SemaphoreType.DMA((NB,)),
            pltpu.SemaphoreType.DMA((7, STEPS)),
            pltpu.SemaphoreType.DMA((7, STEPS)),
            pltpu.SemaphoreType.DMA((STEPS, FOLDS)),
            pltpu.SemaphoreType.DMA((STEPS, 8)),
        ],
        compiler_params=pltpu.CompilerParams(collective_id=1, has_side_effects=True, vmem_limit_bytes=48 << 20),
    )(lam, x, yt, fold)


def tail_kernel(beta_ref, x_ref, fold_ref, old_ref, oof_ref, cross_ref, betas, mine, feats, terms, rows, sums,
                bsend, brecv, fsend, frecv, tsend, trecv, ssend, srecv):
    s, b = lax.axis_index("smp"), lax.axis_index("blk")
    samples = x_ref.shape[0]
    barrier = pltpu.get_barrier_semaphore()

    def greet_smp(i, carry):
        pl.semaphore_signal(barrier, inc=1, device_id={"smp": lax.rem(s + i, 8)}, device_id_type=MESH)
        return carry

    def greet_blk(i, carry):
        pl.semaphore_signal(barrier, inc=1, device_id={"blk": lax.rem(b + i, 16)}, device_id_type=MESH)
        return carry

    lax.fori_loop(1, 8, greet_smp, 0)
    lax.fori_loop(1, 16, greet_blk, 0)
    pl.semaphore_wait(barrier, 22)

    def spread(i):
        return pltpu.make_async_remote_copy(
            src_ref=beta_ref, dst_ref=betas.at[s], send_sem=bsend.at[i], recv_sem=brecv.at[s],
            device_id={"smp": lax.rem(s + i, 8)}, device_id_type=MESH)

    def start_spread(i, carry):
        spread(i).start()
        return carry

    def end_spread(i, carry):
        spread(i).wait_send()
        return carry

    @pl.when(s < FOLDS)
    def _():
        lax.fori_loop(1, 8, start_spread, 0)
        betas[s] = beta_ref[...]

    def beta_in(k, carry):
        @pl.when(s != k)
        def _():
            pltpu.make_async_remote_copy(
                src_ref=beta_ref, dst_ref=betas.at[k], send_sem=bsend.at[0], recv_sem=brecv.at[k],
                device_id={"smp": k}, device_id_type=MESH).wait_recv()
        return carry

    lax.fori_loop(0, FOLDS, beta_in, 0)
    flat = jnp.concatenate([betas[k] for k in range(FOLDS)], axis=0)
    fitted = lax.dot_general(flat, x_ref[...], (((1,), (1,)), ((), ())), preferred_element_type=jnp.float32)
    fold = fold_ref[...]
    chosen = jnp.zeros((16, samples), jnp.float32)
    for k in range(FOLDS):
        chosen = jnp.where(fold == k, fitted[16 * k:16 * k + 16, :], chosen)
    oof = (chosen * math.sqrt(8 * samples / BLOCK)).astype(jnp.bfloat16)
    oof_ref[...] = oof
    for c in range(16):
        mine[c] = oof[:, 128 * c:128 * c + 128]
    feats[b] = mine[b]

    def feature(i):
        to = lax.rem(b + i, 16)
        return pltpu.make_async_remote_copy(
            src_ref=mine.at[to], dst_ref=feats.at[b], send_sem=fsend.at[i], recv_sem=frecv.at[i],
            device_id={"blk": to}, device_id_type=MESH)

    def start_feature(i, carry):
        feature(i).start()
        return carry

    def end_feature(i, carry):
        feature(i).wait()
        return carry

    lax.fori_loop(1, 16, start_feature, 0)
    lax.fori_loop(1, 16, end_feature, 0)
    f = jnp.concatenate([feats[c] for c in range(16)], axis=0)
    nt = (((1,), (1,)), ((), ()))
    against_old = lax.dot_general(f, old_ref[...], nt, preferred_element_type=jnp.float32)
    against_new = lax.dot_general(f, f, nt, preferred_element_type=jnp.float32)
    r = lax.broadcasted_iota(jnp.int32, (256, 256), 0)
    c = lax.broadcasted_iota(jnp.int32, (256, 256), 1)
    row_trait = (r >> 1) & 7
    against_old = jnp.where(row_trait == (c >> 5), against_old, 0.0)
    against_new = jnp.where(row_trait == ((c >> 1) & 7), against_new, 0.0)
    r = lax.broadcasted_iota(jnp.int32, (256, 128), 0)
    c = lax.broadcasted_iota(jnp.int32, (256, 128), 1)
    pick_old = jnp.where((r & 31) == c, 1.0, 0.0)
    pick_new = jnp.where(32 + ((r >> 4) << 1) + (r & 1) == c, 1.0, 0.0)
    total = dot(against_old, pick_old) + dot(against_new, pick_new)
    for k in range(16):
        terms[k] = total[16 * k:16 * k + 16, :]
    rows[b] = terms[b]

    def term(i):
        to = lax.rem(b + i, 16)
        return pltpu.make_async_remote_copy(
            src_ref=terms.at[to], dst_ref=rows.at[b], send_sem=tsend.at[i], recv_sem=trecv.at[i],
            device_id={"blk": to}, device_id_type=MESH)

    def start_term(i, carry):
        term(i).start()
        return carry

    def end_term(i, carry):
        term(i).wait()
        return carry

    lax.fori_loop(1, 16, start_term, 0)
    lax.fori_loop(1, 16, end_term, 0)
    part = rows[0]
    for k in range(1, 16):
        part = part + rows[k]
    sums[s] = part

    def last(i):
        return pltpu.make_async_remote_copy(
            src_ref=sums.at[s], dst_ref=sums.at[s], send_sem=ssend.at[i], recv_sem=srecv.at[i],
            device_id={"smp": lax.rem(s + i, 8)}, device_id_type=MESH)

    def start_last(i, carry):
        last(i).start()
        return carry

    def end_last(i, carry):
        last(i).wait()
        return carry

    lax.fori_loop(1, 8, start_last, 0)
    lax.fori_loop(1, 8, end_last, 0)
    final = sums[0]
    for k in range(1, 8):
        final = final + sums[k]
    cross_ref[...] = final * (1.0 / (8 * samples))

    @pl.when(s < FOLDS)
    def _():
        lax.fori_loop(1, 8, end_spread, 0)


def tail(beta, x, fold, old):
    vmem = pl.BlockSpec(memory_space=pltpu.VMEM)
    dma = pltpu.SemaphoreType.DMA
    return pl.pallas_call(
        tail_kernel,
        out_shape=(jax.ShapeDtypeStruct((16, x.shape[0]), jnp.bfloat16), jax.ShapeDtypeStruct((16, 128), jnp.float32)),
        in_specs=[vmem] * 4,
        out_specs=(vmem, vmem),
        scratch_shapes=[
            pltpu.VMEM((FOLDS, 16, BLOCK), jnp.bfloat16),
            pltpu.VMEM((16, 16, 128), jnp.bfloat16),
            pltpu.VMEM((16, 16, 128), jnp.bfloat16),
            pltpu.VMEM((16, 16, 128), jnp.float32),
            pltpu.VMEM((16, 16, 128), jnp.float32),
            pltpu.VMEM((8, 16, 128), jnp.float32),
            dma((8,)), dma((8,)), dma((16,)), dma((16,)), dma((16,)), dma((16,)), dma((8,)), dma((8,)),
        ],
        compiler_params=pltpu.CompilerParams(collective_id=2, has_side_effects=True, vmem_limit_bytes=40 << 20),
    )(beta, x, fold, old)


def local(x, y, fold, lam, old):
    rows = x.shape[0]
    fold = fold[None, :]
    yt = jnp.pad(y.T, ((0, 8), (0, 0)))
    beta = fit(lam, x, yt, fold)
    before = jnp.transpose(old[0], (1, 2, 0)).reshape(256, 128)
    oof, cross = tail(beta, x, fold, before)
    here = lax.dynamic_slice_in_dim(cross, 8 * lax.axis_index("smp"), 8, 1)
    return jnp.transpose(oof.reshape(TRAITS, 2, rows), (2, 0, 1)), here.reshape(TRAITS, 2, 8)


def solution(mesh):
    return jax.shard_map(
        local,
        mesh=mesh,
        in_specs=(P("smp", "blk"), P("smp", None), P("smp"), P(), P("smp", "blk", None, None)),
        out_specs=(P("smp", None, "blk"), P(None, "blk", "smp")),
        check_vma=False,
    )
```

time: 107 us -> 97.6 us (0.912)
  Pallas kernels: 101 us -> 91.5 us
    pallas_call x2 -> x1, Pallas kernels: 71.7 us -> 62.4 us  [fit(): pl.pallas_call(fit_kernel, out_shape=jax.ShapeDtypeStruct((16, BLOCK), jn...]
    unnamed x10 -> x8, local copies, waits for them, and re-layouts: 2.3 us -> 2.95 us
where the time goes in v4:
time: 97.6 us; the launch traced here: 97.3 us
  Pallas kernels  91.5 us (94%)
  local copies, waits for them, and re-layouts  5.1 us (5%)
    pallas_call x1, Pallas kernels, fit(): pl.pallas_call(fit_kernel, out_shape=jax.ShapeDtypeStruct((16, BLOCK), jn...  62.4 us
    pallas_call x1, Pallas kernels, tail(): pl.pallas_call(tail_kernel, out_shape=(jax.ShapeDtypeStruct((16, x.shape[...  29.1 us
    unnamed x8, local copies, waits for them, and re-layouts  2.95 us

profile of v4, /device:TPU:1, one launch (start us, length us, event | category | flops | bytes accessed | tf_op | source)
XLA Modules:
  0.0 97.3 jit_solution(8067933336879130883)
XLA Ops:
  0.6 0.0 copy-start.1
  0.6 0.8 pad.4.yt_ref
  1.4 0.0 copy-start
  1.4 1.6 %copy-done = bf16[2048,512]{1,0:T(8,128)(2,1)S(1)} copy-done((bf16[2048,512]{1,0:T(8,128)(2,1)S(1)}, bf16[2048,512]{1,0:T(8,128)(2,1)}, u32[]{:S(2)}) %copy-start) | copy-done | bytes 2097176
  3.0 0.0 copy-start.2
  3.0 0.7 copy-done.2
  3.7 0.0 copy-start.3
  3.7 0.7 copy-done.3
  4.4 62.4 %shard_map.68.beta_ref = bf16[16,512]{1,0:T(8,128)(2,1)S(1)} custom-call(f32[2]{0:T(128)S(1)} %copy-done.3, bf16[2048,512]{1,0:T(8,128)(2,1)S(1)} %copy-done, bf16[16,2048]{1,0:T(8,128)(2,1)S(1)} %pad.4.yt_ref, s32[1,2048]{1,0:T(1,128)S(1)} %bitcast.10), custom_call_target="tpu_custom_call" | custom-call | tf_op jit(solution)/shard_map/pallas_call | solution.py:317
  66.8 0.0 copy-done.1
  66.8 29.1 %shard_map.69 = (bf16[16,2048]{1,0:T(8,128)(2,1)S(1)}, f32[16,128]{1,0:T(8,128)S(1)}) custom-call(bf16[16,512]{1,0:T(8,128)(2,1)S(1)} %shard_map.68.beta_ref, bf16[2048,512]{1,0:T(8,128)(2,1)S(1)} %copy-done, s32[1,2048]{1,0:T(1,128)S(1)} %bitcast.11, bf16[256,128]{1,0:T(8,128)(2,1)S(1)} %bitcast.9), custom_call_target="tpu_custom_call" | custom-call | tf_op jit(solution)/shard_map/pallas_call | solution.py:487
  96.0 0.7 constant_dynamic-slice_fusion
  96.6 0.7 reshape.14
Async XLA Ops:
  0.6 66.2 %copy-start.1 = (bf16[1,128,8,32]{1,3,2,0:T(8,128)(2,1)S(1)}, bf16[1,128,8,32]{1,3,2,0:T(8,128)(2,1)}, u32[]{:S(2)}) copy-start(bf16[1,128,8,32]{1,3,2,0:T(8,128)(2,1)} %param.9) | copy-start | bytes 196612
  1.4 1.6 %copy-start = (bf16[2048,512]{1,0:T(8,128)(2,1)S(1)}, bf16[2048,512]{1,0:T(8,128)(2,1)}, u32[]{:S(2)}) copy-start(bf16[2048,512]{1,0:T(8,128)(2,1)} %x_ref.3) | copy-start | bytes 6291460
  3.0 0.7 copy-start.2
  3.7 0.7 copy-start.3

commit v5 on v4

--- a/solution.py
+++ b/solution.py
@@ -101,6 +101,7 @@
 def fit_kernel(lam_ref, x_ref, yt_ref, fold_ref, beta_ref, out_ref, s_ref, t_ref, y_ref, b_ref, xv, lhs, part, relay, plain, comb, half, zin, done,
                 load, send, recv, gsend, grecv):
     me = lax.axis_index("smp")
+    fold_here = lax.rem(3 * me, 8)
     y, z = lax.div(me, 2), lax.rem(me, 2)
     right = lax.rem(y + 1, 4) * 2 + z
     left = lax.rem(y + 3, 4) * 2 + z
@@ -114,10 +115,12 @@
     for i in range(1, 8):
         pl.semaphore_signal(barrier, inc=1, device_id={"smp": lax.rem(me + i, 8)}, device_id_type=MESH)
 
-    @pl.when(me >= FOLDS)
+    @pl.when(fold_here >= FOLDS)
     def _():
         out_ref[...] = jnp.zeros_like(out_ref)
 
+    y_rows = jnp.concatenate([yt_ref[...].astype(jnp.float32), jnp.zeros((8, x_ref.shape[0]), jnp.float32)], axis=0)
+    y_rows = y_rows.astype(jnp.bfloat16)
     masks = [jnp.where(fold_ref[...] != k, 1.0, 0.0).astype(jnp.bfloat16) for k in range(FOLDS)]
     ready = set()
 
@@ -148,7 +151,7 @@
         return pltpu.make_async_remote_copy(
             src_ref=done.at[pl.ds(FOLDS * START[c] + k * ROWS[c], ROWS[c])],
             dst_ref=out_ref.at[sender, pl.ds(START[c], ROWS[c])],
-            send_sem=gsend.at[c, k], recv_sem=grecv.at[c, sender], device_id={"smp": k}, device_id_type=MESH)
+            send_sem=gsend.at[c, k], recv_sem=grecv.at[c, sender], device_id={"smp": 3 * k % 8}, device_id_type=MESH)
 
     def rows_of(p):
         if p in ready:
@@ -180,8 +183,7 @@
         if c == XY_CHUNK:
             for p in range(NB):
                 rows_of(p)
-            yt = yt_ref[...]
-            v = jnp.dot(jnp.concatenate([yt * m for m in masks], axis=0), xv[...], preferred_element_type=jnp.float32)
+            v = jnp.dot(jnp.concatenate([y_rows * m for m in masks], axis=0), xv[...], preferred_element_type=jnp.float32)
             for k in range(FOLDS):
                 r = FOLDS * START[c] + (k + 1) * ROWS[c] - 8
                 for s in range(8):
@@ -190,7 +192,7 @@
                     part[s, r + 4:r + 8, :] = jnp.zeros((4, 128), jnp.float32)
 
     def arrived(g):
-        @pl.when(me < FOLDS)
+        @pl.when(fold_here < FOLDS)
         def _():
             def one(i, carry):
                 gather(g, 0, lax.rem(me + i, 8)).wait_recv()
@@ -213,41 +215,56 @@
                     for j in range(2):
                         y_ref[j, s:s + 1, 128 * q:128 * q + 128] = out_ref[s, XY_PLACE + q:XY_PLACE + q + 1, :]
 
-    def subtract(p, q):
+    def subtract(p, q, first, last):
+        cols = slice(128 * first, 128 * last)
         for j in range(2):
             a = s_ref[j, p, :, 128 * q:128 * q + 128]
-            s_ref[j, q, :, 128 * q:] = s_ref[j, q, :, 128 * q:] - dot(a, t_ref[j, p, :, 128 * q:], 0, 0)
+            s_ref[j, q, :, cols] = s_ref[j, q, :, cols] - dot(a, t_ref[j, p, :, cols], 0, 0)
+
+    def eliminate(p, ws):
+        lo, hi = 128 * p, 128 * p + 128
+        for j in range(2):
+            y = dot(y_ref[j, :, lo:hi], ws[j])
+            y_ref[j, :, lo:hi] = y
+            if p + 1 < NB:
+                right = s_ref[j, p, :, hi:]
+                t_ref[j, p, :, hi:] = dot(ws[j], right)
+                y_ref[j, :, hi:] = y_ref[j, :, hi:] - dot(y, right)
+
+    def diagonal(p):
+        return inverse([s_ref[j, p, :, 128 * p:128 * p + 128] for j in range(2)])
 
     def tasks():
         arrived(0)
-        for p in range(NB):
-            lo, hi = 128 * p, 128 * p + 128
-            for n, ws in enumerate(inverse([s_ref[j, p, :, lo:hi] for j in range(2)])):
-                if n % 8 == 7:
-                    yield None
-            if p == 0:
-                arrived(1)
-            for j in range(2):
-                y = dot(y_ref[j, :, lo:hi], ws[j])
-                y_ref[j, :, lo:hi] = y
-                if p + 1 < NB:
-                    right = s_ref[j, p, :, hi:]
-                    t_ref[j, p, :, hi:] = dot(ws[j], right)
-                    y_ref[j, :, hi:] = y_ref[j, :, hi:] - dot(y, right)
-            if p == 0:
+        for n, ws in enumerate(diagonal(0)):
+            if n == 7:
                 yield None
-                arrived(2)
-                arrived(3)
-                subtract(0, 1)
+        arrived(1)
+        eliminate(0, ws)
+        yield None
+        arrived(2)
+        subtract(0, 1, 1, 3)
+        for n, ws in enumerate(diagonal(1)):
+            if n in (7, 15):
                 yield None
-            elif p == 1:
-                arrived(4)
-                arrived(5)
-                for q in range(2, NB):
-                    subtract(0, q)
-                    subtract(1, q)
-            elif p == 2:
-                subtract(2, 3)
+        arrived(3)
+        subtract(0, 1, 3, 4)
+        eliminate(1, ws)
+        subtract(0, 2, 2, 3)
+        subtract(1, 2, 2, 3)
+        for n, ws in enumerate(diagonal(2)):
+            if n == 7:
+                yield None
+        arrived(4)
+        subtract(0, 2, 3, 4)
+        subtract(1, 2, 3, 4)
+        eliminate(2, ws)
+        arrived(5)
+        for q in range(3):
+            subtract(q, 3, 3, 4)
+        for n, ws in enumerate(diagonal(3)):
+            pass
+        eliminate(3, ws)
         for p in range(NB - 2, -1, -1):
             lo, hi = 128 * p, 128 * p + 128
             for j in range(2):
@@ -288,11 +305,11 @@
             cross_z(g).wait_recv()
             done[span(g)] += zin[span(g)]
             for k in range(FOLDS):
-                @pl.when(me != k)
+                @pl.when(fold_here != k)
                 def _():
                     gather(g, k, me).start()
 
-                @pl.when(me == k)
+                @pl.when(fold_here == k)
                 def _():
                     r = FOLDS * START[g] + k * ROWS[g]
                     out_ref[me, START[g]:START[g] + ROWS[g], :] = done[r:r + ROWS[g], :]
@@ -305,7 +322,7 @@
         for c in relays(g) + plains(g) + combs(g) + [cross_z(g)]:
             c.wait_send()
         for k in range(FOLDS):
-            @pl.when(me != k)
+            @pl.when(fold_here != k)
             def _():
                 gather(g, k, me).wait_send()
 
@@ -340,14 +357,17 @@
             pltpu.SemaphoreType.DMA((STEPS, FOLDS)),
             pltpu.SemaphoreType.DMA((STEPS, 8)),
         ],
-        compiler_params=pltpu.CompilerParams(collective_id=1, has_side_effects=True, vmem_limit_bytes=48 << 20),
+        compiler_params=pltpu.CompilerParams(collective_id=1, has_side_effects=True, vmem_limit_bytes=62 << 20),
     )(lam, x, yt, fold)
 
 
-def tail_kernel(beta_ref, x_ref, fold_ref, old_ref, oof_ref, cross_ref, betas, mine, feats, terms, rows, sums,
-                bsend, brecv, fsend, frecv, tsend, trecv, ssend, srecv):
+def tail_kernel(beta_ref, x_ref, fold_ref, old_ref, oof_ref, cross_ref, xv, betas, mine, feats, terms, rows, sums,
+                load, bsend, brecv, fsend, frecv, tsend, trecv, ssend, srecv):
     s, b = lax.axis_index("smp"), lax.axis_index("blk")
+    fold_here = lax.rem(3 * s, 8)
     samples = x_ref.shape[0]
+    fetch = pltpu.make_async_copy(x_ref, xv, load.at[0])
+    fetch.start()
     barrier = pltpu.get_barrier_semaphore()
 
     def greet_smp(i, carry):
@@ -358,13 +378,16 @@
         pl.semaphore_signal(barrier, inc=1, device_id={"blk": lax.rem(b + i, 16)}, device_id_type=MESH)
         return carry
 
-    lax.fori_loop(1, 8, greet_smp, 0)
-    lax.fori_loop(1, 16, greet_blk, 0)
+    for i in range(1, 8):
+        greet_smp(i, 0)
+    for i in range(1, 16):
+        greet_blk(i, 0)
     pl.semaphore_wait(barrier, 22)
+    fetch.wait()
 
     def spread(i):
         return pltpu.make_async_remote_copy(
-            src_ref=beta_ref, dst_ref=betas.at[s], send_sem=bsend.at[i], recv_sem=brecv.at[s],
+            src_ref=beta_ref, dst_ref=betas.at[fold_here], send_sem=bsend.at[i], recv_sem=brecv.at[fold_here],
             device_id={"smp": lax.rem(s + i, 8)}, device_id_type=MESH)
 
     def start_spread(i, carry):
@@ -375,22 +398,24 @@
         spread(i).wait_send()
         return carry
 
-    @pl.when(s < FOLDS)
+    @pl.when(fold_here < FOLDS)
     def _():
-        lax.fori_loop(1, 8, start_spread, 0)
-        betas[s] = beta_ref[...]
+        for i in range(1, 8):
+            start_spread(i, 0)
+        betas[fold_here] = beta_ref[...]
 
     def beta_in(k, carry):
-        @pl.when(s != k)
+        @pl.when(fold_here != k)
         def _():
             pltpu.make_async_remote_copy(
                 src_ref=beta_ref, dst_ref=betas.at[k], send_sem=bsend.at[0], recv_sem=brecv.at[k],
-                device_id={"smp": k}, device_id_type=MESH).wait_recv()
-        return carry
-
-    lax.fori_loop(0, FOLDS, beta_in, 0)
+                device_id={"smp": lax.rem(s + 1, 8)}, device_id_type=MESH).wait_recv()
+        return carry
+
+    for k in range(FOLDS):
+        beta_in(k, 0)
     flat = jnp.concatenate([betas[k] for k in range(FOLDS)], axis=0)
-    fitted = lax.dot_general(flat, x_ref[...], (((1,), (1,)), ((), ())), preferred_element_type=jnp.float32)
+    fitted = lax.dot_general(flat, xv[...], (((1,), (1,)), ((), ())), preferred_element_type=jnp.float32)
     fold = fold_ref[...]
     chosen = jnp.zeros((16, samples), jnp.float32)
     for k in range(FOLDS):
@@ -415,22 +440,28 @@
         feature(i).wait()
         return carry
 
-    lax.fori_loop(1, 16, start_feature, 0)
-    lax.fori_loop(1, 16, end_feature, 0)
+    for i in range(1, 16):
+        start_feature(i, 0)
+    r = lax.broadcasted_iota(jnp.int32, (256, 512), 0)
+    c = lax.broadcasted_iota(jnp.int32, (256, 512), 1)
+    same = ((r >> 1) & 7) == jnp.where(c < 256, c >> 5, (c >> 1) & 7)
+    r = lax.broadcasted_iota(jnp.int32, (512, 128), 0)
+    c = lax.broadcasted_iota(jnp.int32, (512, 128), 1)
+    place = jnp.where(r < 256, r & 31, 32 + (((r - 256) >> 4) << 1) + (r & 1))
+    pick = jnp.where(place == c, 1.0, 0.0).astype(jnp.bfloat16)
+    for i in range(1, 16):
+        end_feature(i, 0)
     f = jnp.concatenate([feats[c] for c in range(16)], axis=0)
     nt = (((1,), (1,)), ((), ()))
-    against_old = lax.dot_general(f, old_ref[...], nt, preferred_element_type=jnp.float32)
-    against_new = lax.dot_general(f, f, nt, preferred_element_type=jnp.float32)
-    r = lax.broadcasted_iota(jnp.int32, (256, 256), 0)
-    c = lax.broadcasted_iota(jnp.int32, (256, 256), 1)
-    row_trait = (r >> 1) & 7
-    against_old = jnp.where(row_trait == (c >> 5), against_old, 0.0)
-    against_new = jnp.where(row_trait == ((c >> 1) & 7), against_new, 0.0)
-    r = lax.broadcasted_iota(jnp.int32, (256, 128), 0)
-    c = lax.broadcasted_iota(jnp.int32, (256, 128), 1)
-    pick_old = jnp.where((r & 31) == c, 1.0, 0.0)
-    pick_new = jnp.where(32 + ((r >> 4) << 1) + (r & 1) == c, 1.0, 0.0)
-    total = dot(against_old, pick_old) + dot(against_new, pick_new)
+    against = lax.dot_general(f, jnp.concatenate([old_ref[...], f], axis=0), nt, preferred_element_type=jnp.float32)
+    chosen = jnp.where(same, against, 0.0)
+    hi = chosen.astype(jnp.bfloat16)
+    rest = chosen - hi.astype(jnp.float32)
+    mid = rest.astype(jnp.bfloat16)
+    low = (rest - mid.astype(jnp.float32)).astype(jnp.bfloat16)
+    total = jnp.dot(hi, pick, preferred_element_type=jnp.float32)
+    total += jnp.dot(mid, pick, preferred_element_type=jnp.float32)
+    total += jnp.dot(low, pick, preferred_element_type=jnp.float32)
     for k in range(16):
         terms[k] = total[16 * k:16 * k + 16, :]
     rows[b] = terms[b]
@@ -449,8 +480,10 @@
         term(i).wait()
         return carry
 
-    lax.fori_loop(1, 16, start_term, 0)
-    lax.fori_loop(1, 16, end_term, 0)
+    for i in range(1, 16):
+        start_term(i, 0)
+    for i in range(1, 16):
+        end_term(i, 0)
     part = rows[0]
     for k in range(1, 16):
         part = part + rows[k]
@@ -469,16 +502,19 @@
         last(i).wait()
         return carry
 
-    lax.fori_loop(1, 8, start_last, 0)
-    lax.fori_loop(1, 8, end_last, 0)
+    for i in range(1, 8):
+        start_last(i, 0)
+    for i in range(1, 8):
+        end_last(i, 0)
     final = sums[0]
     for k in range(1, 8):
         final = final + sums[k]
     cross_ref[...] = final * (1.0 / (8 * samples))
 
-    @pl.when(s < FOLDS)
+    @pl.when(fold_here < FOLDS)
     def _():
-        lax.fori_loop(1, 8, end_spread, 0)
+        for i in range(1, 8):
+            end_spread(i, 0)
 
 
 def tail(beta, x, fold, old):
@@ -487,26 +523,26 @@
     return pl.pallas_call(
         tail_kernel,
         out_shape=(jax.ShapeDtypeStruct((16, x.shape[0]), jnp.bfloat16), jax.ShapeDtypeStruct((16, 128), jnp.float32)),
-        in_specs=[vmem] * 4,
+        in_specs=[vmem, pl.BlockSpec(memory_space=pltpu.HBM), vmem, vmem],
         out_specs=(vmem, vmem),
         scratch_shapes=[
+            pltpu.VMEM(x.shape, jnp.bfloat16),
             pltpu.VMEM((FOLDS, 16, BLOCK), jnp.bfloat16),
             pltpu.VMEM((16, 16, 128), jnp.bfloat16),
             pltpu.VMEM((16, 16, 128), jnp.bfloat16),
             pltpu.VMEM((16, 16, 128), jnp.float32),
             pltpu.VMEM((16, 16, 128), jnp.float32),
             pltpu.VMEM((8, 16, 128), jnp.float32),
-            dma((8,)), dma((8,)), dma((16,)), dma((16,)), dma((16,)), dma((16,)), dma((8,)), dma((8,)),
+            dma((1,)), dma((8,)), dma((8,)), dma((16,)), dma((16,)), dma((16,)), dma((16,)), dma((8,)), dma((8,)),
         ],
-        compiler_params=pltpu.CompilerParams(collective_id=2, has_side_effects=True, vmem_limit_bytes=40 << 20),
+        compiler_params=pltpu.CompilerParams(collective_id=2, has_side_effects=True, vmem_limit_bytes=62 << 20),
     )(beta, x, fold, old)
 
 
 def local(x, y, fold, lam, old):
     rows = x.shape[0]
     fold = fold[None, :]
-    yt = jnp.pad(y.T, ((0, 8), (0, 0)))
-    beta = fit(lam, x, yt, fold)
+    beta = fit(lam, x, y.T, fold)
     before = jnp.transpose(old[0], (1, 2, 0)).reshape(256, 128)
     oof, cross = tail(beta, x, fold, before)
     here = lax.dynamic_slice_in_dim(cross, 8 * lax.axis_index("smp"), 8, 1)

time: 97.6 us -> 94.1 us (0.964)
  local copies, waits for them, and re-layouts: 5.1 us -> 2.9 us
  Pallas kernels: 91.5 us -> 90.3 us
    unnamed x8 -> x0, local copies, waits for them, and re-layouts: 2.95 us -> none
where the time goes in v5:
time: 94.1 us; the launch traced here: 93.8 us
  Pallas kernels  90.3 us (96%)
  local copies, waits for them, and re-layouts  2.9 us (3%)
    pallas_call x1, Pallas kernels, fit(): pl.pallas_call(fit_kernel, out_shape=jax.ShapeDtypeStruct((16, BLOCK), jn...  61.9 us
    pallas_call x1, Pallas kernels, tail(): pl.pallas_call(tail_kernel, out_shape=(jax.ShapeDtypeStruct((16, x.shape[...  28.3 us

profile of v5, /device:TPU:1, one launch (start us, length us, event | category | flops | bytes accessed | tf_op | source)
XLA Modules:
  0.0 93.8 jit_solution(10274432992649393749)
XLA Ops:
  0.6 61.9 %shard_map.68.beta_ref = bf16[16,512]{1,0:T(8,128)(2,1)} custom-call(f32[2]{0:T(128)} %lam_ref.1, bf16[2048,512]{1,0:T(8,128)(2,1)} %x_ref.3, bf16[8,2048]{1,0:T(8,128)(2,1)} %bitcast.11, s32[1,2048]{1,0:T(1,128)} %bitcast.12), custom_call_target="tpu_custom_call" | custom-call | tf_op jit(solution)/shard_map/pallas_call | solution.py:334
  62.6 28.3 %shard_map.69 = (bf16[16,2048]{1,0:T(8,128)(2,1)}, f32[16,128]{1,0:T(8,128)}) custom-call(bf16[16,512]{1,0:T(8,128)(2,1)} %shard_map.68.beta_ref, bf16[2048,512]{1,0:T(8,128)(2,1)} %x_ref.3, s32[1,2048]{1,0:T(1,128)} %bitcast.13, bf16[256,128]{1,0:T(8,128)(2,1)} %bitcast.9), custom_call_target="tpu_custom_call" | custom-call | tf_op jit(solution)/shard_map/pallas_call | solution.py:523
  90.9 1.4 %constant_dynamic-slice_fusion = f32[16,8]{1,0:T(8,128)} fusion(f32[16,128]{1,0:T(8,128)} %get-tuple-element.5, s32[]{:T(128)S(6)} %select_n.3), kind=kLoop, calls=%fused_computation | loop fusion | bytes 1028 | tf_op jit(solution)/shard_map/dynamic_slice | solution.py:548
  92.3 1.5 %reshape.14 = bf16[8,2,2048]{2,1,0:T(2,128)(2,1)} reshape(bf16[16,2048]{1,0:T(8,128)(2,1)} %get-tuple-element.4) | data formatting | bytes 131072 | tf_op jit(solution)/shard_map/reshape | solution.py:549

commit v6 on v5

--- a/solution.py
+++ b/solution.py
@@ -90,6 +90,8 @@
 CHUNKS = [[0, 1], [2, 3], [4, 5], [6, 7], [8], [9]]
 XY_CHUNK = 1
 FIRST = 4
+Z_FIRST = (4, 5)
+LEAD = 0
 STEPS = len(CHUNKS)
 ROWS = [16 * len(c) + (8 if i == XY_CHUNK else 0) for i, c in enumerate(CHUNKS)]
 START = [sum(ROWS[:i]) for i in range(STEPS)]
@@ -98,14 +100,14 @@
 XY_PLACE = START[XY_CHUNK] + 16 * len(CHUNKS[XY_CHUNK])
 
 
-def fit_kernel(lam_ref, x_ref, yt_ref, fold_ref, beta_ref, out_ref, s_ref, t_ref, y_ref, b_ref, xv, lhs, part, relay, plain, comb, half, zin, done,
+def fit_kernel(lam_ref, x_ref, yt_ref, fold_ref, beta_ref, out_ref, s_ref, t_ref, y_ref, b_ref, xv, lhs, part, relay, plain, comb, half, zin, quarters, done,
                 load, send, recv, gsend, grecv):
     me = lax.axis_index("smp")
     fold_here = lax.rem(3 * me, 8)
     y, z = lax.div(me, 2), lax.rem(me, 2)
     right = lax.rem(y + 1, 4) * 2 + z
     left = lax.rem(y + 3, 4) * 2 + z
-    across = lax.rem(y + 2, 4)
+    across, after, before = lax.rem(y + 2, 4), lax.rem(y + 1, 4), lax.rem(y + 3, 4)
     other = y * 2 + (1 - z)
     barrier = pltpu.get_barrier_semaphore()
     loads = [pltpu.make_async_copy(x_ref.at[:, pl.ds(128 * p, 128)], xv.at[:, pl.ds(128 * p, 128)], load.at[p])
@@ -132,19 +134,30 @@
             src_ref=src, dst_ref=dst, send_sem=send.at[kind, c], recv_sem=recv.at[kind, c],
             device_id={"smp": device}, device_id_type=MESH)
 
+    def both(c):
+        if c in Z_FIRST:
+            n = FOLDS * ROWS[c] // 2
+            return (4 * z, pl.ds(FOLDS * START[c], n)), (4 * z, pl.ds(FOLDS * START[c] + n, n))
+        return (0, span(c)), (4, span(c))
+
     def relays(c):
-        return [hop(0, c, part.at[across * 2, span(c)], relay.at[0, span(c)], right),
-                hop(1, c, part.at[across * 2 + 1, span(c)], relay.at[1, span(c)], left)]
+        (zero, r0), (one, r1) = both(c)
+        return [hop(0, c, part.at[zero + across, r0], relay.at[0, r0], right),
+                hop(1, c, part.at[one + across, r1], relay.at[1, r1], left)]
 
     def plains(c):
-        return [hop(2, c, part.at[lax.rem(y + 1, 4) * 2 + 1, span(c)], plain.at[0, span(c)], right),
-                hop(3, c, part.at[lax.rem(y + 3, 4) * 2, span(c)], plain.at[1, span(c)], left)]
+        (zero, r0), (one, r1) = both(c)
+        return [hop(2, c, part.at[one + after, r1], plain.at[0, r1], right),
+                hop(3, c, part.at[zero + before, r0], plain.at[1, r0], left)]
 
     def combs(c):
-        return [hop(4, c, relay.at[0, span(c)], comb.at[0, span(c)], right),
-                hop(5, c, relay.at[1, span(c)], comb.at[1, span(c)], left)]
+        (zero, r0), (one, r1) = both(c)
+        return [hop(4, c, relay.at[0, r0], comb.at[0, r0], right),
+                hop(5, c, relay.at[1, r1], comb.at[1, r1], left)]
 
     def cross_z(c):
+        if c in Z_FIRST:
+            return hop(6, c, part.at[pl.ds(4 * (1 - z), 4), span(c)], quarters.at[:, span(c)], other)
         return hop(6, c, half.at[span(c)], zin.at[span(c)], other)
 
     def gather(c, k, sender):
@@ -179,7 +192,7 @@
             for k in range(FOLDS):
                 for s in range(8):
                     r = FOLDS * START[c] + k * ROWS[c] + 16 * n
-                    part[s, r:r + 16, :] = v[128 * k + 16 * s:128 * k + 16 * s + 16, :]
+                    part[s % 2 * 4 + s // 2, r:r + 16, :] = v[128 * k + 16 * s:128 * k + 16 * s + 16, :]
         if c == XY_CHUNK:
             for p in range(NB):
                 rows_of(p)
@@ -188,8 +201,8 @@
                 r = FOLDS * START[c] + (k + 1) * ROWS[c] - 8
                 for s in range(8):
                     for q in range(NB):
-                        part[s, r + q:r + q + 1, :] = v[16 * k + s:16 * k + s + 1, 128 * q:128 * q + 128]
-                    part[s, r + 4:r + 8, :] = jnp.zeros((4, 128), jnp.float32)
+                        part[s % 2 * 4 + s // 2, r + q:r + q + 1, :] = v[16 * k + s:16 * k + s + 1, 128 * q:128 * q + 128]
+                    part[s % 2 * 4 + s // 2, r + 4:r + 8, :] = jnp.zeros((4, 128), jnp.float32)
 
     def arrived(g):
         @pl.when(fold_here < FOLDS)
@@ -276,43 +289,69 @@
 
     solving = tasks()
 
+    def send_relays(g):
+        for c in relays(g) + plains(g):
+            c.start()
+
+    def send_combs(g):
+        (zero, r0), (one, r1) = both(g)
+        for c in relays(g):
+            c.wait_recv()
+        relay[0, r0] += part[zero + after, r0]
+        relay[1, r1] += part[one + before, r1]
+        for c in combs(g):
+            c.start()
+
+    def totals(g):
+        (zero, r0), (one, r1) = both(g)
+        for c in plains(g) + combs(g):
+            c.wait_recv()
+        return part[zero + y, r0] + plain[1, r0] + comb[0, r0], part[one + y, r1] + plain[0, r1] + comb[1, r1]
+
+    def send_gathers(g):
+        for k in range(FOLDS):
+            @pl.when(fold_here != k)
+            def _():
+                gather(g, k, me).start()
+
+            @pl.when(fold_here == k)
+            def _():
+                r = FOLDS * START[g] + k * ROWS[g]
+                out_ref[me, START[g]:START[g] + ROWS[g], :] = done[r:r + ROWS[g], :]
+
     for i in range(STEPS + 3):
         if i < STEPS:
-            products(i)
+            if i in Z_FIRST:
+                cross_z(i).wait_recv()
+                for n in range(4):
+                    part[4 * z + n, span(i)] += quarters[n, span(i)]
+            else:
+                products(i)
             if i == 0:
                 pl.semaphore_wait(barrier, 7)
-            for c in relays(i) + plains(i):
-                c.start()
+            send_relays(i)
+            if 0 <= i - LEAD < len(Z_FIRST):
+                products(Z_FIRST[i - LEAD])
+                cross_z(Z_FIRST[i - LEAD]).start()
         if 1 <= i <= STEPS:
-            g = i - 1
-            for c in relays(g):
-                c.wait_recv()
-            relay[0, span(g)] += part[lax.rem(y + 1, 4) * 2, span(g)]
-            relay[1, span(g)] += part[lax.rem(y + 3, 4) * 2 + 1, span(g)]
-            for c in combs(g):
-                c.start()
+            send_combs(i - 1)
         if 2 <= i <= STEPS + 1:
             g = i - 2
-            for c in plains(g) + combs(g):
-                c.wait_recv()
-            zero = part[y * 2, span(g)] + plain[1, span(g)] + comb[0, span(g)]
-            one = part[y * 2 + 1, span(g)] + plain[0, span(g)] + comb[1, span(g)]
-            half[span(g)] = jnp.where(z == 0, one, zero)
-            done[span(g)] = jnp.where(z == 0, zero, one)
-            cross_z(g).start()
-        if i >= 3:
+            zero, one = totals(g)
+            if g in Z_FIRST:
+                n = FOLDS * ROWS[g] // 2
+                done[FOLDS * START[g]:FOLDS * START[g] + n] = zero
+                done[FOLDS * START[g] + n:FOLDS * START[g] + 2 * n] = one
+                send_gathers(g)
+            else:
+                half[span(g)] = jnp.where(z == 0, one, zero)
+                done[span(g)] = jnp.where(z == 0, zero, one)
+                cross_z(g).start()
+        if i >= 3 and i - 3 not in Z_FIRST:
             g = i - 3
             cross_z(g).wait_recv()
             done[span(g)] += zin[span(g)]
-            for k in range(FOLDS):
-                @pl.when(fold_here != k)
-                def _():
-                    gather(g, k, me).start()
-
-                @pl.when(fold_here == k)
-                def _():
-                    r = FOLDS * START[g] + k * ROWS[g]
-                    out_ref[me, START[g]:START[g] + ROWS[g], :] = done[r:r + ROWS[g], :]
+            send_gathers(g)
         if i >= FIRST:
             next(solving)
 
@@ -350,6 +389,7 @@
             pltpu.VMEM((2, rows, 128), f32),
             pltpu.VMEM((rows, 128), f32),
             pltpu.VMEM((rows, 128), f32),
+            pltpu.VMEM((4, rows, 128), f32),
             pltpu.VMEM((rows, 128), f32),
             pltpu.SemaphoreType.DMA((NB,)),
             pltpu.SemaphoreType.DMA((7, STEPS)),

time: 94.1 us -> 90.5 us (0.962)
  Pallas kernels: 90.3 us -> 86.6 us
    pallas_call x1, Pallas kernels: 61.9 us -> 58.4 us  [fit(): pl.pallas_call(fit_kernel, out_shape=jax.ShapeDtypeStruct((16, BLOCK), jn...]
where the time goes in v6:
time: 90.5 us; the launch traced here: 90.2 us
  Pallas kernels  86.6 us (96%)
  local copies, waits for them, and re-layouts  2.9 us (3%)
    pallas_call x1, Pallas kernels, fit(): pl.pallas_call(fit_kernel, out_shape=jax.ShapeDtypeStruct((16, BLOCK), jn...  58.4 us
    pallas_call x1, Pallas kernels, tail(): pl.pallas_call(tail_kernel, out_shape=(jax.ShapeDtypeStruct((16, x.shape[...  28.2 us

profile of v6, /device:TPU:1, one launch (start us, length us, event | category | flops | bytes accessed | tf_op | source)
XLA Modules:
  0.0 90.2 jit_solution(2010644899253792764)
XLA Ops:
  0.6 58.4 %shard_map.68.beta_ref = bf16[16,512]{1,0:T(8,128)(2,1)} custom-call(f32[2]{0:T(128)} %lam_ref.1, bf16[2048,512]{1,0:T(8,128)(2,1)} %x_ref.3, bf16[8,2048]{1,0:T(8,128)(2,1)} %bitcast.11, s32[1,2048]{1,0:T(1,128)} %bitcast.12), custom_call_target="tpu_custom_call" | custom-call | tf_op jit(solution)/shard_map/pallas_call | solution.py:373
  59.1 28.2 %shard_map.69 = (bf16[16,2048]{1,0:T(8,128)(2,1)}, f32[16,128]{1,0:T(8,128)}) custom-call(bf16[16,512]{1,0:T(8,128)(2,1)} %shard_map.68.beta_ref, bf16[2048,512]{1,0:T(8,128)(2,1)} %x_ref.3, s32[1,2048]{1,0:T(1,128)} %bitcast.13, bf16[256,128]{1,0:T(8,128)(2,1)} %bitcast.9), custom_call_target="tpu_custom_call" | custom-call | tf_op jit(solution)/shard_map/pallas_call | solution.py:563
  87.3 1.4 %constant_dynamic-slice_fusion = f32[16,8]{1,0:T(8,128)} fusion(f32[16,128]{1,0:T(8,128)} %get-tuple-element.5, s32[]{:T(128)S(6)} %select_n.3), kind=kLoop, calls=%fused_computation | loop fusion | bytes 1028 | tf_op jit(solution)/shard_map/dynamic_slice | solution.py:588
  88.7 1.5 %reshape.14 = bf16[8,2,2048]{2,1,0:T(2,128)(2,1)} reshape(bf16[16,2048]{1,0:T(8,128)(2,1)} %get-tuple-element.4) | data formatting | bytes 131072 | tf_op jit(solution)/shard_map/reshape | solution.py:589

commit v7 on v6

--- a/solution.py
+++ b/solution.py
@@ -268,13 +268,13 @@
         for n, ws in enumerate(diagonal(2)):
             if n == 7:
                 yield None
-        arrived(4)
-        subtract(0, 2, 3, 4)
-        subtract(1, 2, 3, 4)
+                arrived(4)
+                arrived(5)
+                for q in (2, 3):
+                    subtract(0, q, 3, 4)
+                    subtract(1, q, 3, 4)
         eliminate(2, ws)
-        arrived(5)
-        for q in range(3):
-            subtract(q, 3, 3, 4)
+        subtract(2, 3, 3, 4)
         for n, ws in enumerate(diagonal(3)):
             pass
         eliminate(3, ws)
@@ -401,13 +401,15 @@
     )(lam, x, yt, fold)
 
 
-def tail_kernel(beta_ref, x_ref, fold_ref, old_ref, oof_ref, cross_ref, xv, betas, mine, feats, terms, rows, sums,
+def tail_kernel(beta_ref, x_ref, fold_ref, old_ref, oof_ref, cross_ref, xv, fv, ov, betas, mine, feats, terms, rows, sums,
                 load, bsend, brecv, fsend, frecv, tsend, trecv, ssend, srecv):
     s, b = lax.axis_index("smp"), lax.axis_index("blk")
     fold_here = lax.rem(3 * s, 8)
     samples = x_ref.shape[0]
-    fetch = pltpu.make_async_copy(x_ref, xv, load.at[0])
-    fetch.start()
+    fetches = [pltpu.make_async_copy(x_ref, xv, load.at[0]), pltpu.make_async_copy(fold_ref, fv, load.at[1]),
+               pltpu.make_async_copy(old_ref, ov, load.at[2])]
+    for fetch in fetches:
+        fetch.start()
     barrier = pltpu.get_barrier_semaphore()
 
     def greet_smp(i, carry):
@@ -423,7 +425,6 @@
     for i in range(1, 16):
         greet_blk(i, 0)
     pl.semaphore_wait(barrier, 22)
-    fetch.wait()
 
     def spread(i):
         return pltpu.make_async_remote_copy(
@@ -452,16 +453,17 @@
                 device_id={"smp": lax.rem(s + 1, 8)}, device_id_type=MESH).wait_recv()
         return carry
 
+    for fetch in fetches:
+        fetch.wait()
     for k in range(FOLDS):
         beta_in(k, 0)
     flat = jnp.concatenate([betas[k] for k in range(FOLDS)], axis=0)
     fitted = lax.dot_general(flat, xv[...], (((1,), (1,)), ((), ())), preferred_element_type=jnp.float32)
-    fold = fold_ref[...]
+    fold = fv[...]
     chosen = jnp.zeros((16, samples), jnp.float32)
     for k in range(FOLDS):
         chosen = jnp.where(fold == k, fitted[16 * k:16 * k + 16, :], chosen)
     oof = (chosen * math.sqrt(8 * samples / BLOCK)).astype(jnp.bfloat16)
-    oof_ref[...] = oof
     for c in range(16):
         mine[c] = oof[:, 128 * c:128 * c + 128]
     feats[b] = mine[b]
@@ -477,11 +479,12 @@
         return carry
 
     def end_feature(i, carry):
-        feature(i).wait()
+        feature(i).wait_recv()
         return carry
 
     for i in range(1, 16):
         start_feature(i, 0)
+    oof_ref[...] = oof
     r = lax.broadcasted_iota(jnp.int32, (256, 512), 0)
     c = lax.broadcasted_iota(jnp.int32, (256, 512), 1)
     same = ((r >> 1) & 7) == jnp.where(c < 256, c >> 5, (c >> 1) & 7)
@@ -493,7 +496,7 @@
         end_feature(i, 0)
     f = jnp.concatenate([feats[c] for c in range(16)], axis=0)
     nt = (((1,), (1,)), ((), ()))
-    against = lax.dot_general(f, jnp.concatenate([old_ref[...], f], axis=0), nt, preferred_element_type=jnp.float32)
+    against = lax.dot_general(f, jnp.concatenate([ov[...], f], axis=0), nt, preferred_element_type=jnp.float32)
     chosen = jnp.where(same, against, 0.0)
     hi = chosen.astype(jnp.bfloat16)
     rest = chosen - hi.astype(jnp.float32)
@@ -517,7 +520,7 @@
         return carry
 
     def end_term(i, carry):
-        term(i).wait()
+        term(i).wait_recv()
         return carry
 
     for i in range(1, 16):
@@ -539,7 +542,7 @@
         return carry
 
     def end_last(i, carry):
-        last(i).wait()
+        last(i).wait_recv()
         return carry
 
     for i in range(1, 8):
@@ -550,6 +553,11 @@
     for k in range(1, 8):
         final = final + sums[k]
     cross_ref[...] = final * (1.0 / (8 * samples))
+    for i in range(1, 16):
+        feature(i).wait_send()
+        term(i).wait_send()
+    for i in range(1, 8):
+        last(i).wait_send()
 
     @pl.when(fold_here < FOLDS)
     def _():
@@ -563,17 +571,19 @@
     return pl.pallas_call(
         tail_kernel,
         out_shape=(jax.ShapeDtypeStruct((16, x.shape[0]), jnp.bfloat16), jax.ShapeDtypeStruct((16, 128), jnp.float32)),
-        in_specs=[vmem, pl.BlockSpec(memory_space=pltpu.HBM), vmem, vmem],
+        in_specs=[vmem] + [pl.BlockSpec(memory_space=pltpu.HBM)] * 3,
         out_specs=(vmem, vmem),
         scratch_shapes=[
             pltpu.VMEM(x.shape, jnp.bfloat16),
+            pltpu.VMEM(fold.shape, jnp.int32),
+            pltpu.VMEM(old.shape, jnp.bfloat16),
             pltpu.VMEM((FOLDS, 16, BLOCK), jnp.bfloat16),
             pltpu.VMEM((16, 16, 128), jnp.bfloat16),
             pltpu.VMEM((16, 16, 128), jnp.bfloat16),
             pltpu.VMEM((16, 16, 128), jnp.float32),
             pltpu.VMEM((16, 16, 128), jnp.float32),
             pltpu.VMEM((8, 16, 128), jnp.float32),
-            dma((1,)), dma((8,)), dma((8,)), dma((16,)), dma((16,)), dma((16,)), dma((16,)), dma((8,)), dma((8,)),
+            dma((3,)), dma((8,)), dma((8,)), dma((16,)), dma((16,)), dma((16,)), dma((16,)), dma((8,)), dma((8,)),
         ],
         compiler_params=pltpu.CompilerParams(collective_id=2, has_side_effects=True, vmem_limit_bytes=62 << 20),
     )(beta, x, fold, old)

time: 90.5 us -> 90.3 us (level)
  no operation moved by 1% of the time
where the time goes in v7:
time: 90.3 us; the launch traced here: 90 us
  Pallas kernels  86.4 us (96%)
  local copies, waits for them, and re-layouts  2.9 us (3%)
    pallas_call x1, Pallas kernels, fit(): pl.pallas_call(fit_kernel, out_shape=jax.ShapeDtypeStruct((16, BLOCK), jn...  58.3 us
    pallas_call x1, Pallas kernels, tail(): pl.pallas_call(tail_kernel, out_shape=(jax.ShapeDtypeStruct((16, x.shape[...  28.1 us

profile of v7, /device:TPU:1, one launch (start us, length us, event | category | flops | bytes accessed | tf_op | source)
XLA Modules:
  0.0 90.0 jit_solution(4526562757280850771)
XLA Ops:
  0.6 58.3 %shard_map.68.beta_ref = bf16[16,512]{1,0:T(8,128)(2,1)} custom-call(f32[2]{0:T(128)} %lam_ref.1, bf16[2048,512]{1,0:T(8,128)(2,1)} %x_ref.3, bf16[8,2048]{1,0:T(8,128)(2,1)} %bitcast.11, s32[1,2048]{1,0:T(1,128)} %bitcast.12), custom_call_target="tpu_custom_call" | custom-call | tf_op jit(solution)/shard_map/pallas_call | solution.py:373
  59.0 28.1 %shard_map.69 = (bf16[16,2048]{1,0:T(8,128)(2,1)}, f32[16,128]{1,0:T(8,128)}) custom-call(bf16[16,512]{1,0:T(8,128)(2,1)} %shard_map.68.beta_ref, bf16[2048,512]{1,0:T(8,128)(2,1)} %x_ref.3, s32[1,2048]{1,0:T(1,128)} %bitcast.13, bf16[256,128]{1,0:T(8,128)(2,1)} %bitcast.9), custom_call_target="tpu_custom_call" | custom-call | tf_op jit(solution)/shard_map/pallas_call | solution.py:571
  87.1 1.4 %constant_dynamic-slice_fusion = f32[16,8]{1,0:T(8,128)} fusion(f32[16,128]{1,0:T(8,128)} %get-tuple-element.5, s32[]{:T(128)S(6)} %select_n.3), kind=kLoop, calls=%fused_computation | loop fusion | bytes 1028 | tf_op jit(solution)/shard_map/dynamic_slice | solution.py:598
  88.5 1.5 %reshape.14 = bf16[8,2,2048]{2,1,0:T(2,128)(2,1)} reshape(bf16[16,2048]{1,0:T(8,128)(2,1)} %get-tuple-element.4) | data formatting | bytes 131072 | tf_op jit(solution)/shard_map/reshape | solution.py:599

commit v8 on v7

--- a/solution.py
+++ b/solution.py
@@ -441,7 +441,7 @@
 
     @pl.when(fold_here < FOLDS)
     def _():
-        for i in range(1, 8):
+        for i in (5, 4, 3, 7, 1, 6, 2):
             start_spread(i, 0)
         betas[fold_here] = beta_ref[...]
 
@@ -545,7 +545,7 @@
         last(i).wait_recv()
         return carry
 
-    for i in range(1, 8):
+    for i in (5, 4, 3, 7, 1, 6, 2):
         start_last(i, 0)
     for i in range(1, 8):
         end_last(i, 0)

time: 90.3 us -> 89.7 us (level)
  no operation moved by 1% of the time
where the time goes in v8:
time: 89.7 us; the launch traced here: 89.3 us
  Pallas kernels  85.8 us (96%)
  local copies, waits for them, and re-layouts  2.9 us (3%)
    pallas_call x1, Pallas kernels, fit(): pl.pallas_call(fit_kernel, out_shape=jax.ShapeDtypeStruct((16, BLOCK), jn...  58.3 us
    pallas_call x1, Pallas kernels, tail(): pl.pallas_call(tail_kernel, out_shape=(jax.ShapeDtypeStruct((16, x.shape[...  27.4 us

profile of v8, /device:TPU:1, one launch (start us, length us, event | category | flops | bytes accessed | tf_op | source)
XLA Modules:
  0.0 89.3 jit_solution(14395445060962716609)
XLA Ops:
  0.6 58.3 %shard_map.68.beta_ref = bf16[16,512]{1,0:T(8,128)(2,1)} custom-call(f32[2]{0:T(128)} %lam_ref.1, bf16[2048,512]{1,0:T(8,128)(2,1)} %x_ref.3, bf16[8,2048]{1,0:T(8,128)(2,1)} %bitcast.11, s32[1,2048]{1,0:T(1,128)} %bitcast.12), custom_call_target="tpu_custom_call" | custom-call | tf_op jit(solution)/shard_map/pallas_call | solution.py:373
  59.0 27.4 %shard_map.69 = (bf16[16,2048]{1,0:T(8,128)(2,1)}, f32[16,128]{1,0:T(8,128)}) custom-call(bf16[16,512]{1,0:T(8,128)(2,1)} %shard_map.68.beta_ref, bf16[2048,512]{1,0:T(8,128)(2,1)} %x_ref.3, s32[1,2048]{1,0:T(1,128)} %bitcast.13, bf16[256,128]{1,0:T(8,128)(2,1)} %bitcast.9), custom_call_target="tpu_custom_call" | custom-call | tf_op jit(solution)/shard_map/pallas_call | solution.py:571
  86.4 1.4 %constant_dynamic-slice_fusion = f32[16,8]{1,0:T(8,128)} fusion(f32[16,128]{1,0:T(8,128)} %get-tuple-element.5, s32[]{:T(128)S(6)} %select_n.3), kind=kLoop, calls=%fused_computation | loop fusion | bytes 1028 | tf_op jit(solution)/shard_map/dynamic_slice | solution.py:598
  87.8 1.5 %reshape.14 = bf16[8,2,2048]{2,1,0:T(2,128)(2,1)} reshape(bf16[16,2048]{1,0:T(8,128)(2,1)} %get-tuple-element.4) | data formatting | bytes 131072 | tf_op jit(solution)/shard_map/reshape | solution.py:599
